TPU v7x, 256 devices: a whole 4x4x8 slice. The times are simulated.
256 devices in a mesh: layer: 64 (over z, y, x_lo), row: 2 (over x_hi), col: 2 (over core).
Axes of the slice: x: 4 (x_hi: 2, x_lo: 2; x = x_hi * 2 + x_lo), y: 4, z: 8, core: 2. Of those that a mesh axis runs over, the one named last changes fastest.
Arguments:
- markov: bfloat16 [16384, 16384], P('row', ('layer', 'col')), may hold values from 0.049804688 to 1
- markov_tiles: int32 [256, 256], P('row', ('layer', 'col')), may hold values from 0 to 1, as said below
- slab: bfloat16 [16384, 2048], P(('layer', 'row'), 'col'), may hold values from 0.049804688 to 1
- slab_tiles: int32 [256, 32], P(('layer', 'row'), 'col'), may hold values from 0 to 1, as said below
Outputs:
- inflated: float32 [16384, 2048], P(('row', 'layer'), 'col')
Inputs may be any that keep to these rules, and one draw needn't show every extreme that they name: `markov_tiles`: every diagonal tile of the network matrix is present. `slab_tiles`: tile (c, c) of the slab is present for every slab tile column c.
All inputs are finite; a program needn't handle non-finite values.
Results may differ from a plain program's by a relative error of at most 0.0003.
Values may be sent and summed in bfloat16 or wider, within the bound.
No kernel may reach another device: no remote copies, remote signals or barrier semaphores. Data moves between devices by JAX's collectives and lax.ppermute only.
A program may use at most 128 MiB of HBM per device.

v0:
```python
import functools

import jax
import jax.numpy as jnp
from jax import lax
from jax.experimental import pallas as pl
from jax.experimental.pallas import tpu as pltpu
from jax.sharding import Mesh
from jax.sharding import PartitionSpec as P

NZ, NY, NX = 8, 4, 2
TILE = 64
CAP = 21
SLAB_CAP = 19
PARTS = 1
ALL = ("z", "y", "xl", "xh")
LOW = -2.75
STEP = 13.8 / 65534.0


def lanes(rows):
    return lax.broadcasted_iota(jnp.int32, (rows, 128), 1) < TILE


def mask_kernel(tiles, x_ref, o_ref):
    rows, cols = x_ref.shape
    half = lanes(TILE)
    base = pl.program_id(0) * (rows // TILE)
    for i in range(rows // TILE):
        for g in range(cols // 128):
            keep = jnp.where(half, tiles[base + i, 2 * g], tiles[base + i, 2 * g + 1])
            at = (pl.ds(i * TILE, TILE), pl.ds(g * 128, 128))
            x = x_ref[at].astype(jnp.float32)
            o_ref[at] = jnp.where(keep != 0, x, 0.0).astype(o_ref.dtype)


def masked(x, tiles, block):
    return pl.pallas_call(
        mask_kernel,
        grid=(x.shape[0] // block,),
        in_specs=[
            pl.BlockSpec(memory_space=pltpu.SMEM),
            pl.BlockSpec((block, x.shape[1]), lambda i: (i, 0)),
        ],
        out_specs=pl.BlockSpec((block, x.shape[1]), lambda i: (i, 0)),
        out_shape=jax.ShapeDtypeStruct(x.shape, x.dtype),
        name="mask",
    )(tiles, x)


def halves(x):
    return jnp.concatenate([x[:, TILE:], x[:, :TILE]], axis=1)


def half_masks(dtype):
    left = (lax.broadcasted_iota(jnp.int32, (16, 128), 1) < TILE).astype(jnp.float32)
    return left.astype(dtype), (1.0 - left).astype(dtype)


def keep(f0, f1, dtype):
    return jnp.where(lanes(TILE), f0, f1).astype(jnp.float32).astype(dtype)


def slot_parts(base, slot):
    rows = pl.ds(pl.multiple_of(base + 16 * (slot // 4), 16), 16)
    col = 256 * (slot % 4)
    return tuple((rows, pl.ds(pl.multiple_of(col + 128 * k, 128), 128)) for k in range(2))


def put_pair(ref, base, slot, cap, f0, f1, read):
    left, right = half_masks(ref.dtype)

    @pl.when((f0 > 0) & (slot < cap))
    def _():
        for k, at in enumerate(slot_parts(base, slot)):
            ref[at] = read(2 * k) * left + halves(read(2 * k + 1)) * right

    @pl.when((f1 > 0) & (slot + f0 < cap))
    def _():
        for k, at in enumerate(slot_parts(base, slot + f0)):
            ref[at] = halves(read(2 * k)) * left + read(2 * k + 1) * right


def take_pairs(ref, base, cap, slot, flags, outs):
    left, right = half_masks(ref.dtype)
    loaded = []
    for f0, f1 in flags:
        pair = []
        for f in (f0, f1):
            pair.append([ref[at] for at in slot_parts(base, jnp.minimum(slot, cap - 1))])
            slot = slot + f
        loaded.append(pair)
    for (f0, f1), (a, b), out in zip(flags, loaded, outs):
        zero = jnp.zeros((16, 128), jnp.float32)
        l = left * (zero + f0.astype(jnp.float32)).astype(ref.dtype)
        r = right * (zero + f1.astype(jnp.float32)).astype(ref.dtype)
        for k in range(2):
            out(2 * k, a[k] * l + halves(b[k]) * r)
            out(2 * k + 1, halves(a[k]) * l + b[k] * r)
    return slot


def pack_slab_kernel(tiles, x_ref, o_ref):
    o_ref[...] = jnp.zeros_like(o_ref)
    slot = 0
    row = lax.broadcasted_iota(jnp.int32, (16, 128), 0)
    lane = lax.broadcasted_iota(jnp.int32, (16, 128), 1)
    flags = jnp.zeros((16, 128), jnp.int32)
    for i in range(2):
        for g in range(8):
            f0, f1 = tiles[i, 2 * g], tiles[i, 2 * g + 1]

            def read(q, i=i, g=g):
                return x_ref[pl.ds(i * TILE + 16 * q, 16), pl.ds(g * 128, 128)]

            put_pair(o_ref, 0, slot, SLAB_CAP, f0, f1, read)
            slot = slot + f0 + f1
            for j, f in enumerate((f0, f1)):
                here = (row == i) & (lane == 16 + 2 * g + j)
                flags = jnp.where(here, f, flags)
    o_ref[pl.ds(64, 16), pl.ds(768, 128)] = flags.astype(jnp.float32).astype(o_ref.dtype)


def pack_slab(slab, tiles):
    return pl.pallas_call(
        pack_slab_kernel,
        in_specs=[pl.BlockSpec(memory_space=pltpu.SMEM), pl.BlockSpec(memory_space=pltpu.VMEM)],
        out_specs=pl.BlockSpec(memory_space=pltpu.VMEM),
        out_shape=jax.ShapeDtypeStruct((80, 1024), slab.dtype),
        name="pack_slab",
    )(tiles, slab)


def pack_markov_kernel(tiles, slab_tiles, flags_ref, x_ref, slab_ref, up_ref, down_ref, poison_ref):
    dtype = x_ref.dtype
    z = lax.axis_index("z")
    slab_count = 0
    for i in range(2):
        for j in range(16):
            slab_count = slab_count + slab_tiles[i, j]
    fits = slab_count <= SLAB_CAP
    for ref, sign, reach in ((up_ref, 1, 4), (down_ref, -1, 3)):
        ref[pl.ds(80, 80), :] = slab_ref[...]
        ref[pl.ds(160, 96), :] = jnp.zeros((96, 1024), dtype)

        slot = 0
        for e in range(reach):
            to = lax.rem(z + sign * (e + 1) + NZ, NZ) * 16

            def one(t, slot, ref=ref, to=to):
                f0, f1 = tiles[to + t, 0], tiles[to + t, 1]

                @pl.when(f0 + f1 > 0)
                def _():
                    def read(q):
                        return x_ref[pl.ds(pl.multiple_of((to + t) * TILE + 16 * q, 16), 16), :]

                    put_pair(ref, 160, slot, CAP, f0, f1, read)

                return slot + f0 + f1

            slot = lax.fori_loop(0, 16, one, slot, unroll=4)
        fits = fits & (slot <= CAP)
        for e in range(reach):
            to = lax.rem(z + sign * (e + 1) + NZ, NZ) * 16
            flags = flags_ref[pl.ds(pl.multiple_of(to, 16), 16), :].astype(jnp.float32).astype(dtype)
            ref[pl.ds(240, 16), pl.ds(512 + 128 * e, 2)] = flags
    poison_ref[...] = jnp.full((16, 128), jnp.where(fits, 0.0, jnp.nan), dtype)


def pack_markov(markov, markov_tiles, slab_tiles, slab):
    payload = jax.ShapeDtypeStruct((256, 1024), markov.dtype)
    return pl.pallas_call(
        pack_markov_kernel,
        in_specs=[pl.BlockSpec(memory_space=pltpu.SMEM)] * 2 + [pl.BlockSpec(memory_space=pltpu.VMEM)] * 3,
        out_specs=[pl.BlockSpec(memory_space=pltpu.VMEM)] * 3,
        out_shape=[payload, payload, jax.ShapeDtypeStruct((16, 128), markov.dtype)],
        compiler_params=pltpu.CompilerParams(vmem_limit_bytes=16 * 2**20),
        cost_estimate=pl.CostEstimate(flops=2**23, bytes_accessed=20 * 2**20, transcendentals=0),
        name="pack_markov",
    )(markov_tiles, slab_tiles, markov_tiles, markov, slab)


def own_rows_kernel(tiles, poison_ref, x_ref, o_ref, block, sem):
    dtype = x_ref.dtype
    z = lax.axis_index("z")
    copy = pltpu.make_async_copy(x_ref.at[pl.ds(pl.multiple_of(z * 1024, 1024), 1024), :], block, sem)
    copy.start()
    copy.wait()
    poison = poison_ref[pl.ds(0, 1), :]
    for i in range(16):
        rows = pl.ds(i * TILE, TILE)
        o_ref[0, rows, :] = block[rows, :] * keep(tiles[z * 16 + i, 0], tiles[z * 16 + i, 1], dtype) + poison


def own_rows(markov, markov_tiles, poison):
    return pl.pallas_call(
        own_rows_kernel,
        in_specs=[
            pl.BlockSpec(memory_space=pltpu.SMEM),
            pl.BlockSpec(memory_space=pltpu.VMEM),
            pl.BlockSpec(memory_space=pl.ANY),
        ],
        out_specs=pl.BlockSpec(memory_space=pltpu.VMEM),
        out_shape=jax.ShapeDtypeStruct((1, 1024, 128), markov.dtype),
        scratch_shapes=[pltpu.VMEM((1024, 128), markov.dtype), pltpu.SemaphoreType.DMA],
        cost_estimate=pl.CostEstimate(flops=2**20, bytes_accessed=4 * 2**20, transcendentals=0),
        name="own_rows",
    )(markov_tiles, poison, markov)


def stage_kernel(step, ref, other_ref, later, slabs_ref, token_ref, *rest):
    words, scalars, sem = rest[-3:]
    start = ref.shape[0] - 176
    groups = [ref[pl.ds(start + 160, 16), pl.ds(512 + 128 * e, 128)].astype(jnp.float32) for e in range(max(step, 1))]
    words[pl.ds(0, 16), :] = groups[-1].astype(jnp.int32)
    for k, (slab_ref, base) in enumerate(((ref, start), (other_ref, 0))):
        flags = slab_ref[pl.ds(base + 64, 16), pl.ds(768, 128)].astype(jnp.float32)
        words[pl.ds(16 + 8 * k, 8), :] = flags[:8].astype(jnp.int32)
    before = jnp.zeros((1, 128), jnp.float32)
    for flags in groups[:-1]:
        before = before + jnp.sum(flags, axis=0, keepdims=True)
    words[pl.ds(32, 8), :] = jnp.broadcast_to(before, (8, 128)).astype(jnp.int32)
    copy = pltpu.make_async_copy(words, scalars, sem)
    copy.start()
    token_ref[...] = jnp.zeros(token_ref.shape, token_ref.dtype)
    copy.wait()
    unroll = step > 2
    for h, (source, base) in enumerate(((ref, start), (other_ref, 0))):

        def four(t, slot, h=h, source=source, base=base):
            i, g0 = t // 2, 4 * (t % 2)
            flags, outs = [], []
            for g in range(4):
                word = 16 + 2 * (g0 + g)
                flags.append((scalars[16 + 8 * h + i, word], scalars[16 + 8 * h + i, word + 1]))

                def out(q, x, g=g):
                    rows = pl.ds(pl.multiple_of(i * TILE + 16 * q, 16), 16)
                    slabs_ref[0, h, rows, pl.ds(pl.multiple_of(128 * (g0 + g), 128), 128)] = x

                outs.append(out)
            return take_pairs(source, base, SLAB_CAP, slot, flags, outs)

        lax.fori_loop(0, 4, four, 0, unroll=unroll)
    if step > 0:

        def rows_of_four(t, slot):
            flags, outs = [], []
            for i in range(4):
                flags.append((scalars[4 * t + i, 0], scalars[4 * t + i, 1]))

                def out(q, x, i=i):
                    at = pl.ds(pl.multiple_of((4 * t + i) * TILE + 16 * q, 16), 16)
                    rest[0][0, at, :] = x

                outs.append(out)
            return take_pairs(ref, start + 80, CAP, slot, flags, outs)

        lax.fori_loop(0, 4, rows_of_four, scalars[32, 0] + scalars[32, 1], unroll=unroll)


def stage(step, source, other, later):
    dtype = source.dtype
    shapes = [
        jax.ShapeDtypeStruct((1, 2, 128, 1024), dtype),
        jax.ShapeDtypeStruct((16, 128), dtype),
        jax.ShapeDtypeStruct((1, 1024, 128), dtype),
    ]
    shapes = shapes if step > 0 else shapes[:2]
    return pl.pallas_call(
        functools.partial(stage_kernel, step),
        in_specs=[pl.BlockSpec(memory_space=pltpu.VMEM)] * 2 + [pl.BlockSpec(memory_space=pl.ANY)],
        out_specs=[pl.BlockSpec(memory_space=pltpu.VMEM)] * len(shapes),
        out_shape=shapes,
        scratch_shapes=[
            pltpu.VMEM((40, 128), jnp.int32),
            pltpu.SMEM((40, 128), jnp.int32),
            pltpu.SemaphoreType.DMA,
        ],
        compiler_params=pltpu.CompilerParams(vmem_limit_bytes=16 * 2**20),
        cost_estimate=pl.CostEstimate(flops=2**23, bytes_accessed=100 * 2**20, transcendentals=0),
        name="stage",
    )(source, other, later)


def encode(p):
    code = jnp.round((jnp.log2(jnp.maximum(p, 0.15)) - LOW) * (1.0 / STEP)) - 32767.0
    code = jnp.where(p > 0.0, code, jnp.where(p == 0.0, -32768.0, 32767.0))
    return code.astype(jnp.int32).astype(jnp.int16)


def decode(q):
    f = q.astype(jnp.int32).astype(jnp.float32)
    p = jnp.exp2((f + 32767.0) * STEP + LOW)
    return jnp.where(f > -32768.0, jnp.where(f < 32767.0, p, jnp.inf), 0.0)


def product_kernel(counts, part, first, last, *refs):
    n = len(counts)
    lefts, slabs = (refs[:n], refs[n : 2 * n]), refs[2 * n : 3 * n]
    earlier = None if first else refs[3 * n]
    out_ref, left, right, acc, sems, acc_sems = refs[-6:]
    width = right.shape[1]
    cols = pl.ds(part * width, width)
    same = lax.axis_index("xh") == lax.axis_index("core")
    rows = 256
    copies, accs = [], []

    def copy(src, dst):
        copies.append(pltpu.make_async_copy(src, dst, sems.at[len(copies)]))
        copies[-1].start()

    for other in range(2):
        slot = jnp.where(same, other, 1 - other)
        place = 0
        for i, count in enumerate(counts):
            for k in range(count):
                copy(lefts[other][i].at[k], left.at[:, pl.ds(place + 128 * other, 128)])
                at = pl.ds(pl.multiple_of(place + 128 * slot, 128), 128)
                copy(slabs[i].at[k, other, :, cols], right.at[at, :])
                place += 256
    if not first:
        for m in range(1024 // rows):
            at = pl.ds(m * rows, rows)
            accs.append(pltpu.make_async_copy(earlier.at[at, cols], acc.at[at, :], acc_sems.at[m]))
            accs[-1].start()
    for c in copies:
        c.wait()
    for c in accs:
        c.wait()
    step = width // 4 if first and last else width

    def block(t, _):
        m, c = t // (width // step), lax.rem(t, width // step)
        at = pl.ds(pl.multiple_of(m * rows, rows), rows)
        over = pl.ds(pl.multiple_of(c * step, step), step)
        p = jnp.dot(left[at, :], right[:, over], preferred_element_type=jnp.float32)
        if not first:
            p = p + acc[at, over]
        if last:
            q = encode(p)
            for i in range(rows // 128):
                out_ref[m * (rows // 128) + i, :, over] = q[i * 128 : (i + 1) * 128]
        else:
            out_ref[at, over] = p
        return 0

    lax.fori_loop(0, 1024 // rows * (width // step), block, 0, unroll=2 if last and not first else 1)


def product(left, other_left, right, earlier=None, part=0, parts=1, last=True):
    counts = tuple(x.shape[0] for x in left)
    n, depth, width = len(counts), 256 * sum(counts), 1024 // parts
    operands = [*left, *other_left, *right] + ([] if earlier is None else [earlier])
    if last:
        out = jax.ShapeDtypeStruct((8, 128, width), jnp.int16)
    else:
        out = jax.ShapeDtypeStruct((1024, width), jnp.float32)
    return pl.pallas_call(
        functools.partial(product_kernel, counts, part, earlier is None, last),
        in_specs=[pl.BlockSpec(memory_space=pl.ANY)] * len(operands),
        out_specs=pl.BlockSpec(memory_space=pltpu.VMEM),
        out_shape=out,
        scratch_shapes=[
            pltpu.VMEM((1024, depth), jnp.bfloat16),
            pltpu.VMEM((depth, width), jnp.bfloat16),
            pltpu.VMEM((8 if earlier is None else 1024, width), jnp.float32),
            pltpu.SemaphoreType.DMA((4 * sum(counts),)),
            pltpu.SemaphoreType.DMA((4,)),
        ],
        compiler_params=pltpu.CompilerParams(vmem_limit_bytes=20 * 2**20),
        cost_estimate=pl.CostEstimate(
            flops=2 * 1024 * depth * width, bytes_accessed=10 * 2**20, transcendentals=1024 * width
        ),
        name="product",
    )(*operands)


def square_kernel(q_ref, s_ref, sum_ref):
    def columns(t, _):
        cols = pl.ds(pl.multiple_of(t * 256, 256), 256)
        sums = jnp.zeros((16, 256), jnp.float32)
        for r in range(0, 128, 16):
            rows = pl.ds(r, 16)
            total = decode(q_ref[0, rows, cols])
            for i in range(1, 8):
                total = total + decode(q_ref[i, rows, cols])
            s = total * total
            s_ref[rows, cols] = s
            sums = sums + s
        sums = jnp.sum(sums, axis=0, keepdims=True)[None]
        sum_ref[:, :, cols] = jnp.broadcast_to(sums, (128, 1, 256))
        return 0

    lax.fori_loop(0, s_ref.shape[1] // 256, columns, 0)


def squares(q):
    width = q.shape[2]
    return pl.pallas_call(
        square_kernel,
        in_specs=[pl.BlockSpec(memory_space=pltpu.VMEM)],
        out_specs=[pl.BlockSpec(memory_space=pltpu.VMEM)] * 2,
        out_shape=[jax.ShapeDtypeStruct((128, width), jnp.float32), jax.ShapeDtypeStruct((128, 1, width), jnp.float32)],
        cost_estimate=pl.CostEstimate(flops=2**24, bytes_accessed=10 * 2**20, transcendentals=1024 * width),
        name="squares",
    )(q)


def up(x):
    return lax.ppermute(x, "z", [(i, (i + 1) % NZ) for i in range(NZ)])


def down(x):
    return lax.ppermute(x, "z", [(i, (i - 1) % NZ) for i in range(NZ)])


def across(x):
    return lax.ppermute(x, "xh", [(0, 1), (1, 0)])


def swap_core(x):
    return lax.ppermute(x, "core", [(0, 1), (1, 0)])


def exchange(left, other_left, right, earlier=None):
    parts = []
    for part in range(PARTS):
        codes = product(left, other_left, right, earlier, part, PARTS)
        parts.append(squares(lax.all_to_all(codes, ("y", "xl"), 0, 0, tiled=True)))
    sums = jnp.concatenate([b for _, b in parts], axis=2)
    return [a for a, _ in parts], jnp.sum(lax.all_to_all(sums, ALL, 0, 0, tiled=True), axis=0)


def inflate(squared, sums):
    return jnp.concatenate(squared, axis=1) / (sums / 16384.0 + 1e-06)


def dense(markov, markov_tiles, slab, slab_tiles):
    left = masked(markov, markov_tiles, 128).reshape(NZ, 1024, 128)
    left = lax.all_to_all(left, "z", 0, 0, tiled=True)
    z = lax.axis_index("z")
    own = masked(slab, slab_tiles, 128)
    own = jnp.stack([own, across(own)])

    def gather(k, carry):
        block, blocks = carry
        return down(block), lax.dynamic_update_index_in_dim(blocks, block, lax.rem(z + k, NZ), 0)

    _, right = lax.fori_loop(0, NZ, gather, (own, jnp.zeros((NZ, *own.shape), own.dtype)))
    return inflate(*exchange([left], [swap_core(left)], [right]))


def per_device(markov, markov_tiles, slab, slab_tiles):
    own = pack_slab(slab, slab_tiles)
    other = across(own)
    p, n, poison = pack_markov(markov, markov_tiles, slab_tiles, own)
    p, n = (lax.dynamic_update_slice(x, other, (0, 0)) for x in (p, n))
    lefts = [own_rows(markov, markov_tiles, poison)]
    others = [swap_core(lefts[0])]
    right, token = stage(0, p, p, lefts[0])
    rights = [right]
    for step in range(1, 5):
        if step < 4:
            p, n = up(p), down(n)
            p, n = (lax.dynamic_update_slice(x, token, (240, 256)) for x in (p, n))
            arrived = [(p, p), (n, n)]
        else:
            arrived = [(up(p[80:]), down(n[:80]))]
            token = early = product(lefts[:5], others[:5], rights[:5], last=False)
        for x, other in arrived:
            right, token, left = stage(step, x, other, token)
            lefts.append(left)
            others.append(swap_core(left))
            rights.append(right)
    squared, sums = exchange(lefts[5:], others[5:], rights[5:], early)
    return lax.cond(
        sums[0, 0] < 1e30,
        lambda: inflate(squared, sums),
        lambda: dense(markov, markov_tiles, slab, slab_tiles),
    )


def solution(mesh):
    fine = Mesh(mesh.devices.reshape(NZ, NY, NX, 2, 2), ("z", "y", "xl", "xh", "core"))
    layer = ("z", "y", "xl")
    in_specs = (
        P("xh", layer + ("core",)),
        P("xh", layer + ("core",)),
        P(layer + ("xh",), "core"),
        P(layer + ("xh",), "core"),
    )
    return jax.shard_map(
        per_device, mesh=fine, in_specs=in_specs, out_specs=P(("xh",) + layer, "core"), check_vma=False
    )
```

profile of v0, /device:TPU:2, one launch (start us, length us, event | category | flops | bytes accessed | tf_op | source)
XLA Modules:
  0.0 143.2 jit_solution(14196342796537980576)
XLA Ops:
  0.0 2.6 %pack_slab.1.slab_ref = bf16[80,1024]{1,0:T(8,128)(2,1)} custom-call(s32[2,16]{1,0:T(2,128)} %slab_tiles.1, bf16[128,1024]{1,0:T(8,128)(2,1)} %x_ref.3), custom_call_target="tpu_custom_call" | custom-call | tf_op jit(solution)/shard_map/pack_slab/pallas_call | solution.py:125
  2.6 1.9 %collective-permute-start.3 = (bf16[80,1024]{1,0:T(8,128)(2,1)}, bf16[80,1024]{1,0:T(8,128)(2,1)S(1)}, u32[]{:S(2)}, u32[]{:S(2)}) collective-permute-start(bf16[80,1024]{1,0:T(8,128)(2,1)} %pack_slab.1.slab_ref), channel_id=1, source_target_pairs={{0,2},{2,0},{1,3},{3,1},{4,6},{6,4},{5,7},{7,5},{8,10},{10,8},{9,1... | collective-permute-start | bytes 491528 | tf_op jit(solution)/shard_map/ppermute | solution.py:420
  5.3 0.9 copy-done.3
  6.3 3.5 %pack_markov.1 = (bf16[256,1024]{1,0:T(8,128)(2,1)S(1)}, bf16[256,1024]{1,0:T(8,128)(2,1)S(1)}, bf16[16,128]{1,0:T(8,128)(2,1)S(1)}) custom-call(s32[128,2]{1,0:T(8,128)S(1)} %copy.7.tiles.flags_ref, s32[2,16]{1,0:T(2,128)} %slab_tiles.1, s32[128,2]{1,0:T(8,128)S(1)} %copy.7.tiles.flags_ref, bf16[8192,128]{1,0:T(8,128)(2,1)} %x_ref.5, ...), custom_call_target="tpu_custom_call" | custom-call | flops 8388608 | bytes 20971520 | tf_op jit(solution)/shard_map/pack_markov/pallas_call | solution.py:173
  10.1 2.1 %collective-permute-start.4 = (bf16[256,1024]{1,0:T(8,128)(2,1)S(1)}, bf16[256,1024]{1,0:T(8,128)(2,1)S(1)}, u32[]{:S(2)}, u32[]{:S(2)}) collective-permute-start(bf16[256,1024]{1,0:T(8,128)(2,1)S(1)} %get-tuple-element.173.ref.other_ref), channel_id=1, source_target_pairs={{0,32},{32,64},{64,96},{96,128},{128,160},{160,192},{192,224},{224... | collective-permute-start | bytes 1572872 | tf_op jit(solution)/shard_map/ppermute | solution.py:412
  12.2 4.3 %collective-permute-start.6 = (bf16[256,1024]{1,0:T(8,128)(2,1)S(1)}, bf16[256,1024]{1,0:T(8,128)(2,1)S(1)}, u32[]{:S(2)}, u32[]{:S(2)}) collective-permute-start(bf16[256,1024]{1,0:T(8,128)(2,1)S(1)} %get-tuple-element.172), channel_id=1, source_target_pairs={{0,224},{32,0},{64,32},{96,64},{128,96},{160,128},{192,160},{224,1... | collective-permute-start | bytes 1572872 | tf_op jit(solution)/shard_map/ppermute | solution.py:416
  16.5 3.5 %own_rows.1.later.refs_0_ = bf16[1,1024,128]{2,1,0:T(8,128)(2,1)} custom-call(s32[128,2]{1,0:T(8,128)} %copy-done.2, bf16[16,128]{1,0:T(8,128)(2,1)} %copy-done.4, bf16[8192,128]{1,0:T(8,128)(2,1)} %x_ref.5), custom_call_target="tpu_custom_call" | custom-call | flops 1048576 | bytes 4194304 | tf_op jit(solution)/shard_map/own_rows/pallas_call | solution.py:197
  19.9 0.9 copy-done
  20.9 2.2 %stage.8 = (bf16[1,2,128,1024]{3,2,1,0:T(8,128)(2,1)S(1)}, bf16[16,128]{1,0:T(8,128)(2,1)S(1)}) custom-call(bf16[256,1024]{1,0:T(8,128)(2,1)S(1)} %get-tuple-element.173.ref.other_ref, bf16[256,1024]{1,0:T(8,128)(2,1)S(1)} %get-tuple-element.173.ref.other_ref, bf16[1,1024,128]{2,1,0:T(8,128)(2,1)S(1)} %copy-done), custom_call_target="tpu_custom_call" | custom-call | flops 8388608 | bytes 104857600 | tf_op jit(solution)/shard_map/stage/pallas_call | solution.py:271
  23.1 4.1 %collective-permute-done.4 = bf16[256,1024]{1,0:T(8,128)(2,1)S(1)} collective-permute-done((bf16[256,1024]{1,0:T(8,128)(2,1)S(1)}, bf16[256,1024]{1,0:T(8,128)(2,1)S(1)}, u32[]{:S(2)}, u32[]{:S(2)}) %collective-permute-start.4) | collective-permute-done | bytes 524320 | tf_op jit(solution)/shard_map/ppermute | solution.py:412
  27.3 3.4 %collective-permute-start.8 = (bf16[256,1024]{1,0:T(8,128)(2,1)S(1)}, bf16[256,1024]{1,0:T(8,128)(2,1)S(1)}, u32[]{:S(2)}, u32[]{:S(2)}) collective-permute-start(bf16[256,1024]{1,0:T(8,128)(2,1)S(1)} %get-tuple-element.178.ref.other_ref), channel_id=1, source_target_pairs={{0,224},{32,0},{64,32},{96,64},{128,96},{160,128},{192,160},{224,1... | collective-permute-start | bytes 1572872 | tf_op jit(solution)/shard_map/ppermute | solution.py:416
  30.7 2.8 %stage.9 = (bf16[1,2,128,1024]{3,2,1,0:T(8,128)(2,1)S(1)}, bf16[16,128]{1,0:T(8,128)(2,1)S(1)}, bf16[1,1024,128]{2,1,0:T(8,128)(2,1)S(1)}) custom-call(bf16[256,1024]{1,0:T(8,128)(2,1)S(1)} %get-tuple-element.179.ref.other_ref, bf16[256,1024]{1,0:T(8,128)(2,1)S(1)} %get-tuple-element.179.ref.other_ref, bf16[16,128]{1,0:T(8,128)(2,1)S(1)} %get-tuple-element.135.later), custom_call_target="tpu_custom_call" | custom-call | flops 8388608 | bytes 104857600 | tf_op jit(solution)/shard_map/stage/pallas_call | solution.py:271
  33.4 2.8 %stage.10 = (bf16[1,2,128,1024]{3,2,1,0:T(8,128)(2,1)S(1)}, bf16[16,128]{1,0:T(8,128)(2,1)S(1)}, bf16[1,1024,128]{2,1,0:T(8,128)(2,1)S(1)}) custom-call(bf16[256,1024]{1,0:T(8,128)(2,1)S(1)} %get-tuple-element.178.ref.other_ref, bf16[256,1024]{1,0:T(8,128)(2,1)S(1)} %get-tuple-element.178.ref.other_ref, bf16[16,128]{1,0:T(8,128)(2,1)S(1)} %get-tuple-element.137.later), custom_call_target="tpu_custom_call" | custom-call | flops 8388608 | bytes 104857600 | tf_op jit(solution)/shard_map/stage/pallas_call | solution.py:271
  36.2 4.6 %collective-permute-done.5 = bf16[256,1024]{1,0:T(8,128)(2,1)S(1)} collective-permute-done((bf16[256,1024]{1,0:T(8,128)(2,1)S(1)}, bf16[256,1024]{1,0:T(8,128)(2,1)S(1)}, u32[]{:S(2)}, u32[]{:S(2)}) %collective-permute-start.5) | collective-permute-done | bytes 524320 | tf_op jit(solution)/shard_map/ppermute | solution.py:412
  40.9 2.7 %collective-permute-start.7 = (bf16[256,1024]{1,0:T(8,128)(2,1)S(1)}, bf16[256,1024]{1,0:T(8,128)(2,1)S(1)}, u32[]{:S(2)}, u32[]{:S(2)}) collective-permute-start(bf16[256,1024]{1,0:T(8,128)(2,1)S(1)} %get-tuple-element.177.ref.other_ref), channel_id=1, source_target_pairs={{0,32},{32,64},{64,96},{96,128},{128,160},{160,192},{192,224},{224... | collective-permute-start | bytes 1572872 | tf_op jit(solution)/shard_map/ppermute | solution.py:412
  44.7 2.8 %stage.11 = (bf16[1,2,128,1024]{3,2,1,0:T(8,128)(2,1)S(1)}, bf16[16,128]{1,0:T(8,128)(2,1)S(1)}, bf16[1,1024,128]{2,1,0:T(8,128)(2,1)S(1)}) custom-call(bf16[256,1024]{1,0:T(8,128)(2,1)S(1)} %get-tuple-element.177.ref.other_ref, bf16[256,1024]{1,0:T(8,128)(2,1)S(1)} %get-tuple-element.177.ref.other_ref, bf16[16,128]{1,0:T(8,128)(2,1)S(1)} %get-tuple-element.138.later), custom_call_target="tpu_custom_call" | custom-call | flops 8388608 | bytes 104857600 | tf_op jit(solution)/shard_map/stage/pallas_call | solution.py:271
  47.5 2.8 %stage.12 = (bf16[1,2,128,1024]{3,2,1,0:T(8,128)(2,1)S(1)}, bf16[16,128]{1,0:T(8,128)(2,1)S(1)}, bf16[1,1024,128]{2,1,0:T(8,128)(2,1)S(1)}) custom-call(bf16[256,1024]{1,0:T(8,128)(2,1)S(1)} %get-tuple-element.176.ref.other_ref, bf16[256,1024]{1,0:T(8,128)(2,1)S(1)} %get-tuple-element.176.ref.other_ref, bf16[16,128]{1,0:T(8,128)(2,1)S(1)} %get-tuple-element.139.later), custom_call_target="tpu_custom_call" | custom-call | flops 8388608 | bytes 104857600 | tf_op jit(solution)/shard_map/stage/pallas_call | solution.py:271
  50.3 3.5 %collective-permute-done.7 = bf16[256,1024]{1,0:T(8,128)(2,1)S(1)} collective-permute-done((bf16[256,1024]{1,0:T(8,128)(2,1)S(1)}, bf16[256,1024]{1,0:T(8,128)(2,1)S(1)}, u32[]{:S(2)}, u32[]{:S(2)}) %collective-permute-start.7) | collective-permute-done | bytes 524320 | tf_op jit(solution)/shard_map/ppermute | solution.py:412
  54.7 2.0 %collective-permute-start.10 = (bf16[176,1024]{1,0:T(8,128)(2,1)S(1)}, bf16[176,1024]{1,0:T(8,128)(2,1)S(1)}, u32[]{:S(2)}, u32[]{:S(2)}) collective-permute-start(bf16[176,1024]{1,0:T(8,128)(2,1)S(1)} %slice.12), channel_id=1, source_target_pairs={{0,32},{32,64},{64,96},{96,128},{128,160},{160,192},{192,224},{224... | collective-permute-start | bytes 1081352 | tf_op jit(solution)/shard_map/ppermute | solution.py:412
  56.7 1.4 collective-permute-start.11
  58.1 4.3 %product.4.later.refs_9_ = f32[1024,1024]{1,0:T(8,128)S(1)} custom-call(bf16[1,1024,128]{2,1,0:T(8,128)(2,1)S(1)} %copy-done.1, bf16[1,1024,128]{2,1,0:T(8,128)(2,1)S(1)} %get-tuple-element.144.refs_1_, bf16[1,1024,128]{2,1,0:T(8,128)(2,1)S(1)} %get-tuple-element.145.refs_2_, bf16[1,1024,128]{2,1,0:T(8,128)(2,1)S(1)} %get-tuple-element.146.refs_3_, ...), custom_call_target="tpu_custom_call" | custom-call | flops 2684354560 | bytes 10485760 | tf_op jit(solution)/shard_map/product/pallas_call | solution.py:360
  62.4 2.0 %stage.13 = (bf16[1,2,128,1024]{3,2,1,0:T(8,128)(2,1)S(1)}, bf16[16,128]{1,0:T(8,128)(2,1)S(1)}, bf16[1,1024,128]{2,1,0:T(8,128)(2,1)S(1)}) custom-call(bf16[256,1024]{1,0:T(8,128)(2,1)S(1)} %get-tuple-element.175.ref.other_ref, bf16[256,1024]{1,0:T(8,128)(2,1)S(1)} %get-tuple-element.175.ref.other_ref, bf16[16,128]{1,0:T(8,128)(2,1)S(1)} %get-tuple-element.140.later), custom_call_target="tpu_custom_call" | custom-call | flops 8388608 | bytes 104857600 | tf_op jit(solution)/shard_map/stage/pallas_call | solution.py:271
  64.4 2.5 %stage.14 = (bf16[1,2,128,1024]{3,2,1,0:T(8,128)(2,1)S(1)}, bf16[16,128]{1,0:T(8,128)(2,1)}, bf16[1,1024,128]{2,1,0:T(8,128)(2,1)S(1)}) custom-call(bf16[256,1024]{1,0:T(8,128)(2,1)S(1)} %get-tuple-element.174.ref.other_ref, bf16[256,1024]{1,0:T(8,128)(2,1)S(1)} %get-tuple-element.174.ref.other_ref, bf16[16,128]{1,0:T(8,128)(2,1)S(1)} %get-tuple-element.142.later), custom_call_target="tpu_custom_call" | custom-call | flops 8388608 | bytes 104857600 | tf_op jit(solution)/shard_map/stage/pallas_call | solution.py:271
  67.5 2.5 %stage.15 = (bf16[1,2,128,1024]{3,2,1,0:T(8,128)(2,1)S(1)}, bf16[16,128]{1,0:T(8,128)(2,1)}, bf16[1,1024,128]{2,1,0:T(8,128)(2,1)S(1)}) custom-call(bf16[176,1024]{1,0:T(8,128)(2,1)S(1)} %collective-permute-done.10.ref, bf16[80,1024]{1,0:T(8,128)(2,1)S(1)} %collective-permute-done.11.other_ref, f32[1024,1024]{1,0:T(8,128)S(1)} %product.4.later.refs_9_), custom_call_target="tpu_custom_call" | custom-call | flops 8388608 | bytes 104857600 | tf_op jit(solution)/shard_map/stage/pallas_call | solution.py:271
  70.2 1.4 collective-permute-done.19.refs_5_
  71.6 4.2 %product.5 = s16[8,128,1024]{2,1,0:T(8,128)(2,1)S(1)} custom-call(bf16[1,1024,128]{2,1,0:T(8,128)(2,1)S(1)} %get-tuple-element.141.refs_0_, bf16[1,1024,128]{2,1,0:T(8,128)(2,1)S(1)} %get-tuple-element.143.refs_1_, bf16[1,1024,128]{2,1,0:T(8,128)(2,1)S(1)} %get-tuple-element.153.refs_2_, bf16[1,1024,128]{2,1,0:T(8,128)(2,1)S(1)} %collective-permute-done.17.refs_3_, ...), custom_call_target="tpu_custom_call" | custom-call | flops 1610612736 | bytes 10485760 | tf_op jit(solution)/shard_map/product/pallas_call | solution.py:360
  75.8 32.7 %all_to_all.24.q_ref = s16[8,128,1024]{2,1,0:T(8,128)(2,1)} all-to-all(s16[8,128,1024]{2,1,0:T(8,128)(2,1)S(1)} %product.5), channel_id=1, replica_groups=mesh['z'=8,'y'=4,'xl'=2,'xh'=2,'core'=2] {'y','xl'}, dimensions={0} | all-to-all | bytes 4194304 | tf_op jit(solution)/shard_map/all_to_all | solution.py:431
  108.5 4.2 %squares.3 = (f32[128,1024]{1,0:T(8,128)}, f32[128,1,1024]{2,1,0:T(1,128)}) custom-call(s16[8,128,1024]{2,1,0:T(8,128)(2,1)} %all_to_all.24.q_ref), custom_call_target="tpu_custom_call" | custom-call | flops 16777216 | bytes 10485760 | tf_op jit(solution)/shard_map/squares/pallas_call | solution.py:401
  112.8 8.9 %all-to-all-start.4 = ((f32[128,1,1024]{2,1,0:T(1,128)}), f32[128,1,1024]{2,1,0:T(1,128)S(1)}, u32[]{:S(2)}, u32[]{:S(2)}) async-start(f32[128,1,1024]{2,1,0:T(1,128)} %get-tuple-element.157), calls=%async_computation.4 | async-start | bytes 1048576 | tf_op jit(solution)/shard_map/all_to_all | solution.py:433
  121.7 17.9 %all-to-all-done.4 = f32[128,1,1024]{2,1,0:T(1,128)S(1)} async-done(((f32[128,1,1024]{2,1,0:T(1,128)}), f32[128,1,1024]{2,1,0:T(1,128)S(1)}, u32[]{:S(2)}, u32[]{:S(2)}) %all-to-all-start.4) | async-done | bytes 524320 | tf_op jit(solution)/shard_map/all_to_all | solution.py:433
  141.2 1.1 conditional.1
  141.3 1.1 broadcast_divide_fusion.1
  (51 shorter events, 5.8 us)
Async XLA Ops:
  2.6 7.4 %collective-permute-start.3 = (bf16[80,1024]{1,0:T(8,128)(2,1)}, bf16[80,1024]{1,0:T(8,128)(2,1)S(1)}, u32[]{:S(2)}, u32[]{:S(2)}) collective-permute-start(bf16[80,1024]{1,0:T(8,128)(2,1)} %pack_slab.1.slab_ref), channel_id=1, source_target_pairs={{0,2},{2,0},{1,3},{3,1},{4,6},{6,4},{5,7},{7,5},{8,10},{10,8},{9,1... | collective-permute-start | bytes 491528 | tf_op jit(solution)/shard_map/ppermute | solution.py:420
  5.3 0.9 copy-start.3
  6.3 10.2 %copy-start.2 = (s32[128,2]{1,0:T(8,128)}, s32[128,2]{1,0:T(8,128)S(1)}, u32[]{:S(2)}) copy-start(s32[128,2]{1,0:T(8,128)S(1)} %copy.7.tiles.flags_ref) | copy-start | bytes 3076
  9.7 2.4 %copy-start.4 = (bf16[16,128]{1,0:T(8,128)(2,1)}, bf16[16,128]{1,0:T(8,128)(2,1)S(1)}, u32[]{:S(2)}) copy-start(bf16[16,128]{1,0:T(8,128)(2,1)S(1)} %get-tuple-element.134.poison_ref) | copy-start | bytes 12292
  10.1 17.1 %collective-permute-start.4 = (bf16[256,1024]{1,0:T(8,128)(2,1)S(1)}, bf16[256,1024]{1,0:T(8,128)(2,1)S(1)}, u32[]{:S(2)}, u32[]{:S(2)}) collective-permute-start(bf16[256,1024]{1,0:T(8,128)(2,1)S(1)} %get-tuple-element.173.ref.other_ref), channel_id=1, source_target_pairs={{0,32},{32,64},{64,96},{96,128},{128,160},{160,192},{192,224},{224... | collective-permute-start | bytes 1572872 | tf_op jit(solution)/shard_map/ppermute | solution.py:412
  12.2 15.0 %collective-permute-start.6 = (bf16[256,1024]{1,0:T(8,128)(2,1)S(1)}, bf16[256,1024]{1,0:T(8,128)(2,1)S(1)}, u32[]{:S(2)}, u32[]{:S(2)}) collective-permute-start(bf16[256,1024]{1,0:T(8,128)(2,1)S(1)} %get-tuple-element.172), channel_id=1, source_target_pairs={{0,224},{32,0},{64,32},{96,64},{128,96},{160,128},{192,160},{224,1... | collective-permute-start | bytes 1572872 | tf_op jit(solution)/shard_map/ppermute | solution.py:416
  19.9 1.0 copy-start
  20.9 37.2 %copy-start.1 = (bf16[1,1024,128]{2,1,0:T(8,128)(2,1)S(1)}, bf16[1,1024,128]{2,1,0:T(8,128)(2,1)}, u32[]{:S(2)}) copy-start(bf16[1,1024,128]{2,1,0:T(8,128)(2,1)} %own_rows.1.later.refs_0_) | copy-start | bytes 786436
  27.2 13.6 %collective-permute-start.5 = (bf16[256,1024]{1,0:T(8,128)(2,1)S(1)}, bf16[256,1024]{1,0:T(8,128)(2,1)S(1)}, u32[]{:S(2)}, u32[]{:S(2)}) collective-permute-start(bf16[256,1024]{1,0:T(8,128)(2,1)S(1)} %get-tuple-element.179.ref.other_ref), channel_id=1, source_target_pairs={{0,32},{32,64},{64,96},{96,128},{128,160},{160,192},{192,224},{224... | collective-permute-start | bytes 1572872 | tf_op jit(solution)/shard_map/ppermute | solution.py:412
  27.3 13.6 %collective-permute-start.8 = (bf16[256,1024]{1,0:T(8,128)(2,1)S(1)}, bf16[256,1024]{1,0:T(8,128)(2,1)S(1)}, u32[]{:S(2)}, u32[]{:S(2)}) collective-permute-start(bf16[256,1024]{1,0:T(8,128)(2,1)S(1)} %get-tuple-element.178.ref.other_ref), channel_id=1, source_target_pairs={{0,224},{32,0},{64,32},{96,64},{128,96},{160,128},{192,160},{224,1... | collective-permute-start | bytes 1572872 | tf_op jit(solution)/shard_map/ppermute | solution.py:416
  40.9 12.9 %collective-permute-start.7 = (bf16[256,1024]{1,0:T(8,128)(2,1)S(1)}, bf16[256,1024]{1,0:T(8,128)(2,1)S(1)}, u32[]{:S(2)}, u32[]{:S(2)}) collective-permute-start(bf16[256,1024]{1,0:T(8,128)(2,1)S(1)} %get-tuple-element.177.ref.other_ref), channel_id=1, source_target_pairs={{0,32},{32,64},{64,96},{96,128},{128,160},{160,192},{192,224},{224... | collective-permute-start | bytes 1572872 | tf_op jit(solution)/shard_map/ppermute | solution.py:412
  43.6 11.1 %collective-permute-start.9 = (bf16[256,1024]{1,0:T(8,128)(2,1)S(1)}, bf16[256,1024]{1,0:T(8,128)(2,1)S(1)}, u32[]{:S(2)}, u32[]{:S(2)}) collective-permute-start(bf16[256,1024]{1,0:T(8,128)(2,1)S(1)} %get-tuple-element.176.ref.other_ref), channel_id=1, source_target_pairs={{0,224},{32,0},{64,32},{96,64},{128,96},{160,128},{192,160},{224,1... | collective-permute-start | bytes 1572872 | tf_op jit(solution)/shard_map/ppermute | solution.py:416
  44.2 10.5 %collective-permute-start.12 = (bf16[1,1024,128]{2,1,0:T(8,128)(2,1)}, bf16[1,1024,128]{2,1,0:T(8,128)(2,1)S(1)}, u32[]{:S(2)}, u32[]{:S(2)}) collective-permute-start(bf16[1,1024,128]{2,1,0:T(8,128)(2,1)} %own_rows.1.later.refs_0_), channel_id=1, source_target_pairs={{0,1},{1,0},{2,3},{3,2},{4,5},{5,4},{6,7},{7,6},{8,9},{9,8},{10,11... | collective-permute-start | bytes 786440 | tf_op jit(solution)/shard_map/ppermute | solution.py:424
  44.2 12.5 %collective-permute-start.14 = (bf16[1,1024,128]{2,1,0:T(8,128)(2,1)S(1)}, bf16[1,1024,128]{2,1,0:T(8,128)(2,1)S(1)}, u32[]{:S(2)}, u32[]{:S(2)}) collective-permute-start(bf16[1,1024,128]{2,1,0:T(8,128)(2,1)S(1)} %get-tuple-element.145.refs_2_), channel_id=1, source_target_pairs={{0,1},{1,0},{2,3},{3,2},{4,5},{5,4},{6,7},{7,6},{8,9},{9,8},{10,11... | collective-permute-start | bytes 786440 | tf_op jit(solution)/shard_map/ppermute | solution.py:424
  44.7 13.4 %collective-permute-start.13 = (bf16[1,1024,128]{2,1,0:T(8,128)(2,1)S(1)}, bf16[1,1024,128]{2,1,0:T(8,128)(2,1)S(1)}, u32[]{:S(2)}, u32[]{:S(2)}) collective-permute-start(bf16[1,1024,128]{2,1,0:T(8,128)(2,1)S(1)} %get-tuple-element.144.refs_1_), channel_id=1, source_target_pairs={{0,1},{1,0},{2,3},{3,2},{4,5},{5,4},{6,7},{7,6},{8,9},{9,8},{10,11... | collective-permute-start | bytes 786440 | tf_op jit(solution)/shard_map/ppermute | solution.py:424
  53.8 4.3 %collective-permute-start.16 = (bf16[1,1024,128]{2,1,0:T(8,128)(2,1)S(1)}, bf16[1,1024,128]{2,1,0:T(8,128)(2,1)S(1)}, u32[]{:S(2)}, u32[]{:S(2)}) collective-permute-start(bf16[1,1024,128]{2,1,0:T(8,128)(2,1)S(1)} %get-tuple-element.147.refs_4_), channel_id=1, source_target_pairs={{0,1},{1,0},{2,3},{3,2},{4,5},{5,4},{6,7},{7,6},{8,9},{9,8},{10,11... | collective-permute-start | bytes 786440 | tf_op jit(solution)/shard_map/ppermute | solution.py:424
  54.6 3.5 %collective-permute-start.15 = (bf16[1,1024,128]{2,1,0:T(8,128)(2,1)S(1)}, bf16[1,1024,128]{2,1,0:T(8,128)(2,1)S(1)}, u32[]{:S(2)}, u32[]{:S(2)}) collective-permute-start(bf16[1,1024,128]{2,1,0:T(8,128)(2,1)S(1)} %get-tuple-element.146.refs_3_), channel_id=1, source_target_pairs={{0,1},{1,0},{2,3},{3,2},{4,5},{5,4},{6,7},{7,6},{8,9},{9,8},{10,11... | collective-permute-start | bytes 786440 | tf_op jit(solution)/shard_map/ppermute | solution.py:424
  54.7 12.8 %collective-permute-start.10 = (bf16[176,1024]{1,0:T(8,128)(2,1)S(1)}, bf16[176,1024]{1,0:T(8,128)(2,1)S(1)}, u32[]{:S(2)}, u32[]{:S(2)}) collective-permute-start(bf16[176,1024]{1,0:T(8,128)(2,1)S(1)} %slice.12), channel_id=1, source_target_pairs={{0,32},{32,64},{64,96},{96,128},{128,160},{160,192},{192,224},{224... | collective-permute-start | bytes 1081352 | tf_op jit(solution)/shard_map/ppermute | solution.py:412
  56.7 10.8 %collective-permute-start.11 = (bf16[80,1024]{1,0:T(8,128)(2,1)S(1)}, bf16[80,1024]{1,0:T(8,128)(2,1)S(1)}, u32[]{:S(2)}, u32[]{:S(2)}) collective-permute-start(bf16[80,1024]{1,0:T(8,128)(2,1)S(1)} %slice.13), channel_id=1, source_target_pairs={{0,224},{32,0},{64,32},{96,64},{128,96},{160,128},{192,160},{224,1... | collective-permute-start | bytes 491528 | tf_op jit(solution)/shard_map/ppermute | solution.py:416
  66.9 3.3 %collective-permute-start.18 = (bf16[1,1024,128]{2,1,0:T(8,128)(2,1)S(1)}, bf16[1,1024,128]{2,1,0:T(8,128)(2,1)S(1)}, u32[]{:S(2)}, u32[]{:S(2)}) collective-permute-start(bf16[1,1024,128]{2,1,0:T(8,128)(2,1)S(1)} %get-tuple-element.143.refs_1_), channel_id=1, source_target_pairs={{0,1},{1,0},{2,3},{3,2},{4,5},{5,4},{6,7},{7,6},{8,9},{9,8},{10,11... | collective-permute-start | bytes 786440 | tf_op jit(solution)/shard_map/ppermute | solution.py:424
  67.0 3.2 %collective-permute-start.17 = (bf16[1,1024,128]{2,1,0:T(8,128)(2,1)S(1)}, bf16[1,1024,128]{2,1,0:T(8,128)(2,1)S(1)}, u32[]{:S(2)}, u32[]{:S(2)}) collective-permute-start(bf16[1,1024,128]{2,1,0:T(8,128)(2,1)S(1)} %get-tuple-element.141.refs_0_), channel_id=1, source_target_pairs={{0,1},{1,0},{2,3},{3,2},{4,5},{5,4},{6,7},{7,6},{8,9},{9,8},{10,11... | collective-permute-start | bytes 786440 | tf_op jit(solution)/shard_map/ppermute | solution.py:424
  70.0 1.6 %collective-permute-start.19 = (bf16[1,1024,128]{2,1,0:T(8,128)(2,1)S(1)}, bf16[1,1024,128]{2,1,0:T(8,128)(2,1)S(1)}, u32[]{:S(2)}, u32[]{:S(2)}) collective-permute-start(bf16[1,1024,128]{2,1,0:T(8,128)(2,1)S(1)} %get-tuple-element.153.refs_2_), channel_id=1, source_target_pairs={{0,1},{1,0},{2,3},{3,2},{4,5},{5,4},{6,7},{7,6},{8,9},{9,8},{10,11... | collective-permute-start | bytes 786440 | tf_op jit(solution)/shard_map/ppermute | solution.py:424
  75.8 65.4 %copy-start.5 = (bf16[8192,128]{1,0:T(8,128)(2,1)S(1)}, bf16[8192,128]{1,0:T(8,128)(2,1)}, u32[]{:S(2)}) copy-start(bf16[8192,128]{1,0:T(8,128)(2,1)} %x_ref.5) | copy-start | bytes 6291460
  75.8 65.4 %copy-start.6 = (bf16[128,1024]{1,0:T(8,128)(2,1)S(1)}, bf16[128,1024]{1,0:T(8,128)(2,1)}, u32[]{:S(2)}) copy-start(bf16[128,1024]{1,0:T(8,128)(2,1)} %x_ref.3) | copy-start | bytes 786436
  75.8 65.4 %copy-start.8 = (s32[2,16]{1,0:T(2,128)S(1)}, s32[2,16]{1,0:T(2,128)}, u32[]{:S(2)}) copy-start(s32[2,16]{1,0:T(2,128)} %slab_tiles.1) | copy-start | bytes 388
  75.8 65.4 %copy-start.9 = (s32[128,2]{0,1:T(2,128)S(1)}, s32[128,2]{0,1:T(2,128)}, u32[]{:S(2)}) copy-start(s32[128,2]{0,1:T(2,128)} %param.9) | copy-start | bytes 3076
  112.8 26.8 %all-to-all-start.4 = ((f32[128,1,1024]{2,1,0:T(1,128)}), f32[128,1,1024]{2,1,0:T(1,128)S(1)}, u32[]{:S(2)}, u32[]{:S(2)}) async-start(f32[128,1,1024]{2,1,0:T(1,128)} %get-tuple-element.157), calls=%async_computation.4 | async-start | bytes 1048576 | tf_op jit(solution)/shard_map/all_to_all | solution.py:433
  142.4 0.8 copy-start.7
where the time goes:
time: 145 us; the launch traced here: 143 us
  Pallas kernels  42.5 us (29%)
  waiting for transfers between devices  32.8 us (23%)
  blocking collectives  32.7 us (23%)
  starting transfers between devices  28.6 us (20%)
  local copies, waits for them, and re-layouts  4.13 us (3%)
  other arithmetic  1.45 us (1%)
    all_to_all x1, blocking collectives, exchange(): parts.append(squares(lax.all_to_all(codes, ('y', 'xl'), 0, 0, tiled=True)))  32.7 us
    pallas_call x8, Pallas kernels, stage(): pl.pallas_call(functools.partial(stage_kernel, step), in_specs=[pl.BlockS...  20.2 us
    all_to_all x1, waiting for transfers between devices, exchange(): lax.all_to_all(sums, ALL, 0, 0, tiled=True)  17.9 us
    ppermute x4, waiting for transfers between devices, up(): return lax.ppermute(x, 'z', [(i, (i + 1) % NZ) for i in range(NZ)])  12.2 us
    ppermute x4, starting transfers between devices, down(): return lax.ppermute(x, 'z', [(i, (i - 1) % NZ) for i in range(NZ)])  9.7 us
    all_to_all x1, starting transfers between devices, exchange(): lax.all_to_all(sums, ALL, 0, 0, tiled=True)  8.9 us
    pallas_call x2, Pallas kernels, product(): pl.pallas_call(functools.partial(product_kernel, counts, part, earlier is...  8.46 us
    ppermute x4, starting transfers between devices, up(): return lax.ppermute(x, 'z', [(i, (i + 1) % NZ) for i in range(NZ)])  6.8 us
  transfers between devices with their start and end apart: 18, of which 8 were waited for; matrix products, arithmetic and copies ran while one was open for 1% of the time, Pallas kernels for 22%

commit v1 on v0

--- a/solution.py
+++ b/solution.py
@@ -131,7 +131,7 @@
     )(tiles, slab)
 
 
-def pack_markov_kernel(tiles, slab_tiles, flags_ref, x_ref, slab_ref, up_ref, down_ref, poison_ref):
+def pack_markov_kernel(tiles, slab_tiles, flags_ref, x_ref, slab_ref, up_ref, down_ref, poison_ref, sems):
     dtype = x_ref.dtype
     z = lax.axis_index("z")
     slab_count = 0
@@ -139,8 +139,12 @@
         for j in range(16):
             slab_count = slab_count + slab_tiles[i, j]
     fits = slab_count <= SLAB_CAP
+    copies = [
+        pltpu.make_async_copy(slab_ref, ref.at[pl.ds(80, 80), :], sems.at[k]) for k, ref in enumerate((up_ref, down_ref))
+    ]
+    for c in copies:
+        c.start()
     for ref, sign, reach in ((up_ref, 1, 4), (down_ref, -1, 3)):
-        ref[pl.ds(80, 80), :] = slab_ref[...]
         ref[pl.ds(160, 96), :] = jnp.zeros((96, 1024), dtype)
 
         slot = 0
@@ -165,6 +169,8 @@
             to = lax.rem(z + sign * (e + 1) + NZ, NZ) * 16
             flags = flags_ref[pl.ds(pl.multiple_of(to, 16), 16), :].astype(jnp.float32).astype(dtype)
             ref[pl.ds(240, 16), pl.ds(512 + 128 * e, 2)] = flags
+    for c in copies:
+        c.wait()
     poison_ref[...] = jnp.full((16, 128), jnp.where(fits, 0.0, jnp.nan), dtype)
 
 
@@ -172,9 +178,12 @@
     payload = jax.ShapeDtypeStruct((256, 1024), markov.dtype)
     return pl.pallas_call(
         pack_markov_kernel,
-        in_specs=[pl.BlockSpec(memory_space=pltpu.SMEM)] * 2 + [pl.BlockSpec(memory_space=pltpu.VMEM)] * 3,
+        in_specs=[pl.BlockSpec(memory_space=pltpu.SMEM)] * 2
+        + [pl.BlockSpec(memory_space=pltpu.VMEM)] * 2
+        + [pl.BlockSpec(memory_space=pl.ANY)],
         out_specs=[pl.BlockSpec(memory_space=pltpu.VMEM)] * 3,
         out_shape=[payload, payload, jax.ShapeDtypeStruct((16, 128), markov.dtype)],
+        scratch_shapes=[pltpu.SemaphoreType.DMA((2,))],
         compiler_params=pltpu.CompilerParams(vmem_limit_bytes=16 * 2**20),
         cost_estimate=pl.CostEstimate(flops=2**23, bytes_accessed=20 * 2**20, transcendentals=0),
         name="pack_markov",
@@ -225,7 +234,7 @@
     copy.start()
     token_ref[...] = jnp.zeros(token_ref.shape, token_ref.dtype)
     copy.wait()
-    unroll = step > 2
+    unroll = step > 2 or ref.shape[0] == 176
     for h, (source, base) in enumerate(((ref, start), (other_ref, 0))):
 
         def four(t, slot, h=h, source=source, base=base):
@@ -282,6 +291,46 @@
         cost_estimate=pl.CostEstimate(flops=2**23, bytes_accessed=100 * 2**20, transcendentals=0),
         name="stage",
     )(source, other, later)
+
+
+def last_left_kernel(step, ref, later, left_ref, words, scalars, sem):
+    start = ref.shape[0] - 176
+    groups = [ref[pl.ds(start + 160, 16), pl.ds(512 + 128 * e, 128)].astype(jnp.float32) for e in range(step)]
+    words[pl.ds(0, 16), :] = groups[-1].astype(jnp.int32)
+    before = jnp.zeros((1, 128), jnp.float32)
+    for flags in groups[:-1]:
+        before = before + jnp.sum(flags, axis=0, keepdims=True)
+    words[pl.ds(16, 8), :] = jnp.broadcast_to(before, (8, 128)).astype(jnp.int32)
+    copy = pltpu.make_async_copy(words, scalars, sem)
+    copy.start()
+    copy.wait()
+    slot = scalars[16, 0] + scalars[16, 1]
+    for t in range(4):
+        flags, outs = [], []
+        for i in range(4 * t, 4 * t + 4):
+            flags.append((scalars[i, 0], scalars[i, 1]))
+
+            def out(q, x, i=i):
+                left_ref[0, pl.ds(i * TILE + 16 * q, 16), :] = x
+
+            outs.append(out)
+        slot = take_pairs(ref, start + 80, CAP, slot, flags, outs)
+
+
+def last_left(step, source, later):
+    return pl.pallas_call(
+        functools.partial(last_left_kernel, step),
+        in_specs=[pl.BlockSpec(memory_space=pltpu.VMEM), pl.BlockSpec(memory_space=pl.ANY)],
+        out_specs=pl.BlockSpec(memory_space=pltpu.VMEM),
+        out_shape=jax.ShapeDtypeStruct((1, 1024, 128), source.dtype),
+        scratch_shapes=[
+            pltpu.VMEM((24, 128), jnp.int32),
+            pltpu.SMEM((24, 128), jnp.int32),
+            pltpu.SemaphoreType.DMA,
+        ],
+        cost_estimate=pl.CostEstimate(flops=2**20, bytes_accessed=2 * 2**20, transcendentals=0),
+        name="last_left",
+    )(source, later)
 
 
 def encode(p):
@@ -470,7 +519,11 @@
             arrived = [(up(p[80:]), down(n[:80]))]
             token = early = product(lefts[:5], others[:5], rights[:5], last=False)
         for x, other in arrived:
-            right, token, left = stage(step, x, other, token)
+            if step < 4:
+                right, token, left = stage(step, x, other, token)
+            else:
+                left = last_left(step, x, token)
+                right, token = stage(0, x, other, left)
             lefts.append(left)
             others.append(swap_core(left))
             rights.append(right)

time: 145 us -> 159 us (1.097)
  local copies, waits for them, and re-layouts: 4.13 us -> 11.8 us
  waiting for transfers between devices: 32.8 us -> 37 us
  Pallas kernels: 42.5 us -> 45.4 us
  blocking collectives: 32.7 us -> 31 us
    unnamed x21 -> x33, local copies, waits for them, and re-layouts: 3.47 us -> 11.2 us
    ppermute x4, starting transfers between devices: 6.8 us -> 2.91 us  [up(): return lax.ppermute(x, 'z', [(i, (i + 1) % NZ) for i in range(NZ)])]
    ppermute x4, waiting for transfers between devices: 0.94 us -> 3.98 us  [down(): return lax.ppermute(x, 'z', [(i, (i - 1) % NZ) for i in range(NZ)])]
    pallas_call x0 -> x1, Pallas kernels: none -> 2.87 us  [last_left(): pl.pallas_call(functools.partial(last_left_kernel, step), in_specs=[pl.Bl...]
    ppermute x4, starting transfers between devices: 9.7 us -> 12.6 us  [down(): return lax.ppermute(x, 'z', [(i, (i - 1) % NZ) for i in range(NZ)])]
    ppermute x4, waiting for transfers between devices: 12.2 us -> 14.7 us  [up(): return lax.ppermute(x, 'z', [(i, (i + 1) % NZ) for i in range(NZ)])]
    all_to_all x1, blocking collectives: 32.7 us -> 31 us  [exchange(): parts.append(squares(lax.all_to_all(codes, ('y', 'xl'), 0, 0, tiled=True)))]
  transfers between devices with their start and end apart: 18 -> 18, of which waited for: 8 -> 7; matrix products, arithmetic and copies ran while one was open for 1% -> 1% of each run, Pallas kernels for 22% -> 22%
where the time goes in v1:
time: 159 us; the launch traced here: 157 us
  Pallas kernels  45.4 us (29%)
  waiting for transfers between devices  37 us (23%)
  blocking collectives  31 us (19%)
  starting transfers between devices  29.2 us (18%)
  local copies, waits for them, and re-layouts  11.8 us (7%)
    all_to_all x1, blocking collectives, exchange(): parts.append(squares(lax.all_to_all(codes, ('y', 'xl'), 0, 0, tiled=True)))  31 us
    pallas_call x8, Pallas kernels, stage(): pl.pallas_call(functools.partial(stage_kernel, step), in_specs=[pl.BlockS...  19.9 us
    all_to_all x1, waiting for transfers between devices, exchange(): lax.all_to_all(sums, ALL, 0, 0, tiled=True)  17.1 us
    ppermute x4, waiting for transfers between devices, up(): return lax.ppermute(x, 'z', [(i, (i + 1) % NZ) for i in range(NZ)])  14.7 us
    ppermute x4, starting transfers between devices, down(): return lax.ppermute(x, 'z', [(i, (i - 1) % NZ) for i in range(NZ)])  12.6 us
    unnamed x33, local copies, waits for them, and re-layouts  11.2 us
    all_to_all x1, starting transfers between devices, exchange(): lax.all_to_all(sums, ALL, 0, 0, tiled=True)  9.6 us
    pallas_call x2, Pallas kernels, product(): pl.pallas_call(functools.partial(product_kernel, counts, part, earlier is...  8.44 us
  transfers between devices with their start and end apart: 18, of which 7 were waited for; matrix products, arithmetic and copies ran while one was open for 1% of the time, Pallas kernels for 22%

profile of v1, /device:TPU:2, one launch (start us, length us, event | category | flops | bytes accessed | tf_op | source)
XLA Modules:
  0.0 156.8 jit_solution(8131577165397281724)
XLA Ops:
  0.0 2.5 %pack_slab.1.slab_ref = bf16[80,1024]{1,0:T(8,128)(2,1)} custom-call(s32[2,16]{1,0:T(2,128)} %slab_tiles.1, bf16[128,1024]{1,0:T(8,128)(2,1)} %x_ref.3), custom_call_target="tpu_custom_call" | custom-call | tf_op jit(solution)/shard_map/pack_slab/pallas_call | solution.py:125
  2.5 2.2 %collective-permute-start.3 = (bf16[80,1024]{1,0:T(8,128)(2,1)}, bf16[80,1024]{1,0:T(8,128)(2,1)S(1)}, u32[]{:S(2)}, u32[]{:S(2)}) collective-permute-start(bf16[80,1024]{1,0:T(8,128)(2,1)} %pack_slab.1.slab_ref), channel_id=1, source_target_pairs={{0,2},{2,0},{1,3},{3,1},{4,6},{6,4},{5,7},{7,5},{8,10},{10,8},{9,1... | collective-permute-start | bytes 491528 | tf_op jit(solution)/shard_map/ppermute | solution.py:469
  6.4 4.1 %pack_markov.1 = (bf16[256,1024]{1,0:T(8,128)(2,1)S(1)}, bf16[256,1024]{1,0:T(8,128)(2,1)S(1)}, bf16[16,128]{1,0:T(8,128)(2,1)S(1)}) custom-call(s32[128,2]{1,0:T(8,128)S(1)} %copy.7.tiles.flags_ref, s32[2,16]{1,0:T(2,128)} %slab_tiles.1, s32[128,2]{1,0:T(8,128)S(1)} %copy.7.tiles.flags_ref, bf16[8192,128]{1,0:T(8,128)(2,1)} %x_ref.5, ...), custom_call_target="tpu_custom_call" | custom-call | flops 8388608 | bytes 20971520 | tf_op jit(solution)/shard_map/pack_markov/pallas_call | solution.py:179
  10.6 1.8 %collective-permute-start.4 = (bf16[256,1024]{1,0:T(8,128)(2,1)S(1)}, bf16[256,1024]{1,0:T(8,128)(2,1)S(1)}, u32[]{:S(2)}, u32[]{:S(2)}) collective-permute-start(bf16[256,1024]{1,0:T(8,128)(2,1)S(1)} %get-tuple-element.171.ref.other_ref), channel_id=1, source_target_pairs={{0,32},{32,64},{64,96},{96,128},{128,160},{160,192},{192,224},{224... | collective-permute-start | bytes 1572872 | tf_op jit(solution)/shard_map/ppermute | solution.py:461
  12.4 4.1 %collective-permute-start.6 = (bf16[256,1024]{1,0:T(8,128)(2,1)S(1)}, bf16[256,1024]{1,0:T(8,128)(2,1)S(1)}, u32[]{:S(2)}, u32[]{:S(2)}) collective-permute-start(bf16[256,1024]{1,0:T(8,128)(2,1)S(1)} %get-tuple-element.170), channel_id=1, source_target_pairs={{0,224},{32,0},{64,32},{96,64},{128,96},{160,128},{192,160},{224,1... | collective-permute-start | bytes 1572872 | tf_op jit(solution)/shard_map/ppermute | solution.py:465
  16.5 3.5 %own_rows.1.later.refs_0_ = bf16[1,1024,128]{2,1,0:T(8,128)(2,1)} custom-call(s32[128,2]{1,0:T(8,128)} %copy-done.8, bf16[16,128]{1,0:T(8,128)(2,1)} %copy-done.10, bf16[8192,128]{1,0:T(8,128)(2,1)} %x_ref.5), custom_call_target="tpu_custom_call" | custom-call | flops 1048576 | bytes 4194304 | tf_op jit(solution)/shard_map/own_rows/pallas_call | solution.py:206
  20.9 2.2 %stage.8 = (bf16[1,2,128,1024]{3,2,1,0:T(8,128)(2,1)S(1)}, bf16[16,128]{1,0:T(8,128)(2,1)S(1)}) custom-call(bf16[256,1024]{1,0:T(8,128)(2,1)S(1)} %get-tuple-element.171.ref.other_ref, bf16[256,1024]{1,0:T(8,128)(2,1)S(1)} %get-tuple-element.171.ref.other_ref, bf16[1,1024,128]{2,1,0:T(8,128)(2,1)S(1)} %copy-done.6), custom_call_target="tpu_custom_call" | custom-call | flops 8388608 | bytes 104857600 | tf_op jit(solution)/shard_map/stage/pallas_call | solution.py:280
  23.1 5.0 %collective-permute-done.4 = bf16[256,1024]{1,0:T(8,128)(2,1)S(1)} collective-permute-done((bf16[256,1024]{1,0:T(8,128)(2,1)S(1)}, bf16[256,1024]{1,0:T(8,128)(2,1)S(1)}, u32[]{:S(2)}, u32[]{:S(2)}) %collective-permute-start.4) | collective-permute-done | bytes 524320 | tf_op jit(solution)/shard_map/ppermute | solution.py:461
  28.2 3.4 %collective-permute-start.8 = (bf16[256,1024]{1,0:T(8,128)(2,1)S(1)}, bf16[256,1024]{1,0:T(8,128)(2,1)S(1)}, u32[]{:S(2)}, u32[]{:S(2)}) collective-permute-start(bf16[256,1024]{1,0:T(8,128)(2,1)S(1)} %get-tuple-element.176.ref.other_ref), channel_id=1, source_target_pairs={{0,224},{32,0},{64,32},{96,64},{128,96},{160,128},{192,160},{224,1... | collective-permute-start | bytes 1572872 | tf_op jit(solution)/shard_map/ppermute | solution.py:465
  31.6 2.8 %stage.9 = (bf16[1,2,128,1024]{3,2,1,0:T(8,128)(2,1)S(1)}, bf16[16,128]{1,0:T(8,128)(2,1)S(1)}, bf16[1,1024,128]{2,1,0:T(8,128)(2,1)S(1)}) custom-call(bf16[256,1024]{1,0:T(8,128)(2,1)S(1)} %get-tuple-element.177.ref.other_ref, bf16[256,1024]{1,0:T(8,128)(2,1)S(1)} %get-tuple-element.177.ref.other_ref, bf16[16,128]{1,0:T(8,128)(2,1)S(1)} %get-tuple-element.134.later), custom_call_target="tpu_custom_call" | custom-call | flops 8388608 | bytes 104857600 | tf_op jit(solution)/shard_map/stage/pallas_call | solution.py:280
  34.4 2.8 %stage.10 = (bf16[1,2,128,1024]{3,2,1,0:T(8,128)(2,1)S(1)}, bf16[16,128]{1,0:T(8,128)(2,1)S(1)}, bf16[1,1024,128]{2,1,0:T(8,128)(2,1)S(1)}) custom-call(bf16[256,1024]{1,0:T(8,128)(2,1)S(1)} %get-tuple-element.176.ref.other_ref, bf16[256,1024]{1,0:T(8,128)(2,1)S(1)} %get-tuple-element.176.ref.other_ref, bf16[16,128]{1,0:T(8,128)(2,1)S(1)} %get-tuple-element.136.later), custom_call_target="tpu_custom_call" | custom-call | flops 8388608 | bytes 104857600 | tf_op jit(solution)/shard_map/stage/pallas_call | solution.py:280
  37.2 5.5 %collective-permute-done.5 = bf16[256,1024]{1,0:T(8,128)(2,1)S(1)} collective-permute-done((bf16[256,1024]{1,0:T(8,128)(2,1)S(1)}, bf16[256,1024]{1,0:T(8,128)(2,1)S(1)}, u32[]{:S(2)}, u32[]{:S(2)}) %collective-permute-start.5) | collective-permute-done | bytes 524320 | tf_op jit(solution)/shard_map/ppermute | solution.py:461
  43.6 2.4 %collective-permute-start.9 = (bf16[256,1024]{1,0:T(8,128)(2,1)S(1)}, bf16[256,1024]{1,0:T(8,128)(2,1)S(1)}, u32[]{:S(2)}, u32[]{:S(2)}) collective-permute-start(bf16[256,1024]{1,0:T(8,128)(2,1)S(1)} %get-tuple-element.174.ref.other_ref), channel_id=1, source_target_pairs={{0,224},{32,0},{64,32},{96,64},{128,96},{160,128},{192,160},{224,1... | collective-permute-start | bytes 1572872 | tf_op jit(solution)/shard_map/ppermute | solution.py:465
  46.5 2.8 %stage.11 = (bf16[1,2,128,1024]{3,2,1,0:T(8,128)(2,1)S(1)}, bf16[16,128]{1,0:T(8,128)(2,1)S(1)}, bf16[1,1024,128]{2,1,0:T(8,128)(2,1)S(1)}) custom-call(bf16[256,1024]{1,0:T(8,128)(2,1)S(1)} %get-tuple-element.175.ref.other_ref, bf16[256,1024]{1,0:T(8,128)(2,1)S(1)} %get-tuple-element.175.ref.other_ref, bf16[16,128]{1,0:T(8,128)(2,1)S(1)} %get-tuple-element.137.later), custom_call_target="tpu_custom_call" | custom-call | flops 8388608 | bytes 104857600 | tf_op jit(solution)/shard_map/stage/pallas_call | solution.py:280
  49.3 2.8 %stage.12 = (bf16[1,2,128,1024]{3,2,1,0:T(8,128)(2,1)S(1)}, bf16[16,128]{1,0:T(8,128)(2,1)S(1)}, bf16[1,1024,128]{2,1,0:T(8,128)(2,1)S(1)}) custom-call(bf16[256,1024]{1,0:T(8,128)(2,1)S(1)} %get-tuple-element.174.ref.other_ref, bf16[256,1024]{1,0:T(8,128)(2,1)S(1)} %get-tuple-element.174.ref.other_ref, bf16[16,128]{1,0:T(8,128)(2,1)S(1)} %get-tuple-element.138.later), custom_call_target="tpu_custom_call" | custom-call | flops 8388608 | bytes 104857600 | tf_op jit(solution)/shard_map/stage/pallas_call | solution.py:280
  52.1 4.2 %collective-permute-done.7 = bf16[256,1024]{1,0:T(8,128)(2,1)S(1)} collective-permute-done((bf16[256,1024]{1,0:T(8,128)(2,1)S(1)}, bf16[256,1024]{1,0:T(8,128)(2,1)S(1)}, u32[]{:S(2)}, u32[]{:S(2)}) %collective-permute-start.7) | collective-permute-done | bytes 524320 | tf_op jit(solution)/shard_map/ppermute | solution.py:461
  58.2 4.3 %product.4.later.refs_9_ = f32[1024,1024]{1,0:T(8,128)S(1)} custom-call(bf16[1,1024,128]{2,1,0:T(8,128)(2,1)S(1)} %copy-done.7, bf16[1,1024,128]{2,1,0:T(8,128)(2,1)S(1)} %get-tuple-element.143.refs_1_, bf16[1,1024,128]{2,1,0:T(8,128)(2,1)S(1)} %get-tuple-element.144.refs_2_, bf16[1,1024,128]{2,1,0:T(8,128)(2,1)S(1)} %get-tuple-element.145.refs_3_, ...), custom_call_target="tpu_custom_call" | custom-call | flops 2684354560 | bytes 10485760 | tf_op jit(solution)/shard_map/product/pallas_call | solution.py:409
  62.5 2.0 %copy-done = f32[1024,1024]{1,0:T(8,128)} copy-done((f32[1024,1024]{1,0:T(8,128)}, f32[1024,1024]{1,0:T(8,128)S(1)}, u32[]{:S(2)}) %copy-start) | copy-done | bytes 4194328
  64.5 2.0 %stage.13 = (bf16[1,2,128,1024]{3,2,1,0:T(8,128)(2,1)S(1)}, bf16[16,128]{1,0:T(8,128)(2,1)S(1)}, bf16[1,1024,128]{2,1,0:T(8,128)(2,1)S(1)}) custom-call(bf16[256,1024]{1,0:T(8,128)(2,1)S(1)} %get-tuple-element.173.ref.other_ref, bf16[256,1024]{1,0:T(8,128)(2,1)S(1)} %get-tuple-element.173.ref.other_ref, bf16[16,128]{1,0:T(8,128)(2,1)S(1)} %get-tuple-element.139.later), custom_call_target="tpu_custom_call" | custom-call | flops 8388608 | bytes 104857600 | tf_op jit(solution)/shard_map/stage/pallas_call | solution.py:280
  66.4 2.5 %stage.14 = (bf16[1,2,128,1024]{3,2,1,0:T(8,128)(2,1)S(1)}, bf16[16,128]{1,0:T(8,128)(2,1)}, bf16[1,1024,128]{2,1,0:T(8,128)(2,1)S(1)}) custom-call(bf16[256,1024]{1,0:T(8,128)(2,1)S(1)} %get-tuple-element.172.ref.other_ref, bf16[256,1024]{1,0:T(8,128)(2,1)S(1)} %get-tuple-element.172.ref.other_ref, bf16[16,128]{1,0:T(8,128)(2,1)S(1)} %get-tuple-element.141.later), custom_call_target="tpu_custom_call" | custom-call | flops 8388608 | bytes 104857600 | tf_op jit(solution)/shard_map/stage/pallas_call | solution.py:280
  70.3 2.9 %last_left.1.later.refs_2_ = bf16[1,1024,128]{2,1,0:T(8,128)(2,1)} custom-call(bf16[176,1024]{1,0:T(8,128)(2,1)} %copy-done.4, f32[1024,1024]{1,0:T(8,128)} %copy-done), custom_call_target="tpu_custom_call" | custom-call | flops 1048576 | bytes 2097152 | tf_op jit(solution)/shard_map/last_left/pallas_call | solution.py:321
  73.4 2.7 %collective-permute-start.19 = (bf16[80,1024]{1,0:T(8,128)(2,1)S(1)}, bf16[80,1024]{1,0:T(8,128)(2,1)S(1)}, u32[]{:S(2)}, u32[]{:S(2)}) collective-permute-start(bf16[80,1024]{1,0:T(8,128)(2,1)S(1)} %slice.13), channel_id=1, source_target_pairs={{0,224},{32,0},{64,32},{96,64},{128,96},{160,128},{192,160},{224,1... | collective-permute-start | bytes 491528 | tf_op jit(solution)/shard_map/ppermute | solution.py:465
  76.0 4.0 %collective-permute-done.19.other_ref = bf16[80,1024]{1,0:T(8,128)(2,1)S(1)} collective-permute-done((bf16[80,1024]{1,0:T(8,128)(2,1)S(1)}, bf16[80,1024]{1,0:T(8,128)(2,1)S(1)}, u32[]{:S(2)}, u32[]{:S(2)}) %collective-permute-start.19) | collective-permute-done | bytes 163872 | tf_op jit(solution)/shard_map/ppermute | solution.py:465
  82.0 2.1 %stage.15 = (bf16[1,2,128,1024]{3,2,1,0:T(8,128)(2,1)S(1)}, bf16[16,128]{1,0:T(8,128)(2,1)}) custom-call(bf16[176,1024]{1,0:T(8,128)(2,1)S(1)} %copy-done.5, bf16[80,1024]{1,0:T(8,128)(2,1)S(1)} %collective-permute-done.19.other_ref, bf16[1,1024,128]{2,1,0:T(8,128)(2,1)S(1)} %copy-done.2), custom_call_target="tpu_custom_call" | custom-call | flops 8388608 | bytes 104857600 | tf_op jit(solution)/shard_map/stage/pallas_call | solution.py:280
  84.1 2.2 %copy-done.1 = f32[1024,1024]{1,0:T(8,128)S(1)} copy-done((f32[1024,1024]{1,0:T(8,128)S(1)}, f32[1024,1024]{1,0:T(8,128)}, u32[]{:S(2)}) %copy-start.1) | copy-done | bytes 4194328
  87.3 4.2 %product.5 = s16[8,128,1024]{2,1,0:T(8,128)(2,1)S(1)} custom-call(bf16[1,1024,128]{2,1,0:T(8,128)(2,1)S(1)} %get-tuple-element.140.refs_0_, bf16[1,1024,128]{2,1,0:T(8,128)(2,1)S(1)} %get-tuple-element.142.refs_1_, bf16[1,1024,128]{2,1,0:T(8,128)(2,1)S(1)} %copy-done.3, bf16[1,1024,128]{2,1,0:T(8,128)(2,1)S(1)} %collective-permute-done.16.refs_3_, ...), custom_call_target="tpu_custom_call" | custom-call | flops 1610612736 | bytes 10485760 | tf_op jit(solution)/shard_map/product/pallas_call | solution.py:409
  91.5 31.0 %all_to_all.24.q_ref = s16[8,128,1024]{2,1,0:T(8,128)(2,1)} all-to-all(s16[8,128,1024]{2,1,0:T(8,128)(2,1)S(1)} %product.5), channel_id=1, replica_groups=mesh['z'=8,'y'=4,'xl'=2,'xh'=2,'core'=2] {'y','xl'}, dimensions={0} | all-to-all | bytes 4194304 | tf_op jit(solution)/shard_map/all_to_all | solution.py:480
  122.5 4.2 %squares.3 = (f32[128,1024]{1,0:T(8,128)}, f32[128,1,1024]{2,1,0:T(1,128)}) custom-call(s16[8,128,1024]{2,1,0:T(8,128)(2,1)} %all_to_all.24.q_ref), custom_call_target="tpu_custom_call" | custom-call | flops 16777216 | bytes 10485760 | tf_op jit(solution)/shard_map/squares/pallas_call | solution.py:450
  126.7 9.6 %all-to-all-start.4 = ((f32[128,1,1024]{2,1,0:T(1,128)}), f32[128,1,1024]{2,1,0:T(1,128)S(1)}, u32[]{:S(2)}, u32[]{:S(2)}) async-start(f32[128,1,1024]{2,1,0:T(1,128)} %get-tuple-element.155), calls=%async_computation.4 | async-start | bytes 1048576 | tf_op jit(solution)/shard_map/all_to_all | solution.py:482
  136.3 17.1 %all-to-all-done.4 = f32[128,1,1024]{2,1,0:T(1,128)S(1)} async-done(((f32[128,1,1024]{2,1,0:T(1,128)}), f32[128,1,1024]{2,1,0:T(1,128)S(1)}, u32[]{:S(2)}, u32[]{:S(2)}) %all-to-all-start.4) | async-done | bytes 524320 | tf_op jit(solution)/shard_map/all_to_all | solution.py:482
  154.9 1.1 conditional.1
  154.9 1.1 broadcast_divide_fusion.1
  (64 shorter events, 12.2 us)
Async XLA Ops:
  2.5 8.1 %collective-permute-start.3 = (bf16[80,1024]{1,0:T(8,128)(2,1)}, bf16[80,1024]{1,0:T(8,128)(2,1)S(1)}, u32[]{:S(2)}, u32[]{:S(2)}) collective-permute-start(bf16[80,1024]{1,0:T(8,128)(2,1)} %pack_slab.1.slab_ref), channel_id=1, source_target_pairs={{0,2},{2,0},{1,3},{3,1},{4,6},{6,4},{5,7},{7,5},{8,10},{10,8},{9,1... | collective-permute-start | bytes 491528 | tf_op jit(solution)/shard_map/ppermute | solution.py:469
  5.5 0.9 copy-start.9
  6.4 10.1 %copy-start.8 = (s32[128,2]{1,0:T(8,128)}, s32[128,2]{1,0:T(8,128)S(1)}, u32[]{:S(2)}) copy-start(s32[128,2]{1,0:T(8,128)S(1)} %copy.7.tiles.flags_ref) | copy-start | bytes 3076
  10.5 1.9 %copy-start.10 = (bf16[16,128]{1,0:T(8,128)(2,1)}, bf16[16,128]{1,0:T(8,128)(2,1)S(1)}, u32[]{:S(2)}) copy-start(bf16[16,128]{1,0:T(8,128)(2,1)S(1)} %get-tuple-element.133.poison_ref) | copy-start | bytes 12292
  10.6 17.5 %collective-permute-start.4 = (bf16[256,1024]{1,0:T(8,128)(2,1)S(1)}, bf16[256,1024]{1,0:T(8,128)(2,1)S(1)}, u32[]{:S(2)}, u32[]{:S(2)}) collective-permute-start(bf16[256,1024]{1,0:T(8,128)(2,1)S(1)} %get-tuple-element.171.ref.other_ref), channel_id=1, source_target_pairs={{0,32},{32,64},{64,96},{96,128},{128,160},{160,192},{192,224},{224... | collective-permute-start | bytes 1572872 | tf_op jit(solution)/shard_map/ppermute | solution.py:461
  12.4 15.7 %collective-permute-start.6 = (bf16[256,1024]{1,0:T(8,128)(2,1)S(1)}, bf16[256,1024]{1,0:T(8,128)(2,1)S(1)}, u32[]{:S(2)}, u32[]{:S(2)}) collective-permute-start(bf16[256,1024]{1,0:T(8,128)(2,1)S(1)} %get-tuple-element.170), channel_id=1, source_target_pairs={{0,224},{32,0},{64,32},{96,64},{128,96},{160,128},{192,160},{224,1... | collective-permute-start | bytes 1572872 | tf_op jit(solution)/shard_map/ppermute | solution.py:465
  20.0 1.0 copy-start.6
  20.9 37.3 %copy-start.7 = (bf16[1,1024,128]{2,1,0:T(8,128)(2,1)S(1)}, bf16[1,1024,128]{2,1,0:T(8,128)(2,1)}, u32[]{:S(2)}) copy-start(bf16[1,1024,128]{2,1,0:T(8,128)(2,1)} %own_rows.1.later.refs_0_) | copy-start | bytes 786436
  28.1 14.6 %collective-permute-start.5 = (bf16[256,1024]{1,0:T(8,128)(2,1)S(1)}, bf16[256,1024]{1,0:T(8,128)(2,1)S(1)}, u32[]{:S(2)}, u32[]{:S(2)}) collective-permute-start(bf16[256,1024]{1,0:T(8,128)(2,1)S(1)} %get-tuple-element.177.ref.other_ref), channel_id=1, source_target_pairs={{0,32},{32,64},{64,96},{96,128},{128,160},{160,192},{192,224},{224... | collective-permute-start | bytes 1572872 | tf_op jit(solution)/shard_map/ppermute | solution.py:461
  28.2 14.5 %collective-permute-start.8 = (bf16[256,1024]{1,0:T(8,128)(2,1)S(1)}, bf16[256,1024]{1,0:T(8,128)(2,1)S(1)}, u32[]{:S(2)}, u32[]{:S(2)}) collective-permute-start(bf16[256,1024]{1,0:T(8,128)(2,1)S(1)} %get-tuple-element.176.ref.other_ref), channel_id=1, source_target_pairs={{0,224},{32,0},{64,32},{96,64},{128,96},{160,128},{192,160},{224,1... | collective-permute-start | bytes 1572872 | tf_op jit(solution)/shard_map/ppermute | solution.py:465
  42.7 13.6 %collective-permute-start.7 = (bf16[256,1024]{1,0:T(8,128)(2,1)S(1)}, bf16[256,1024]{1,0:T(8,128)(2,1)S(1)}, u32[]{:S(2)}, u32[]{:S(2)}) collective-permute-start(bf16[256,1024]{1,0:T(8,128)(2,1)S(1)} %get-tuple-element.175.ref.other_ref), channel_id=1, source_target_pairs={{0,32},{32,64},{64,96},{96,128},{128,160},{160,192},{192,224},{224... | collective-permute-start | bytes 1572872 | tf_op jit(solution)/shard_map/ppermute | solution.py:461
  43.6 12.6 %collective-permute-start.9 = (bf16[256,1024]{1,0:T(8,128)(2,1)S(1)}, bf16[256,1024]{1,0:T(8,128)(2,1)S(1)}, u32[]{:S(2)}, u32[]{:S(2)}) collective-permute-start(bf16[256,1024]{1,0:T(8,128)(2,1)S(1)} %get-tuple-element.174.ref.other_ref), channel_id=1, source_target_pairs={{0,224},{32,0},{64,32},{96,64},{128,96},{160,128},{192,160},{224,1... | collective-permute-start | bytes 1572872 | tf_op jit(solution)/shard_map/ppermute | solution.py:465
  46.0 10.8 %collective-permute-start.11 = (bf16[1,1024,128]{2,1,0:T(8,128)(2,1)}, bf16[1,1024,128]{2,1,0:T(8,128)(2,1)S(1)}, u32[]{:S(2)}, u32[]{:S(2)}) collective-permute-start(bf16[1,1024,128]{2,1,0:T(8,128)(2,1)} %own_rows.1.later.refs_0_), channel_id=1, source_target_pairs={{0,1},{1,0},{2,3},{3,2},{4,5},{5,4},{6,7},{7,6},{8,9},{9,8},{10,11... | collective-permute-start | bytes 786440 | tf_op jit(solution)/shard_map/ppermute | solution.py:473
  46.0 10.9 %collective-permute-start.13 = (bf16[1,1024,128]{2,1,0:T(8,128)(2,1)S(1)}, bf16[1,1024,128]{2,1,0:T(8,128)(2,1)S(1)}, u32[]{:S(2)}, u32[]{:S(2)}) collective-permute-start(bf16[1,1024,128]{2,1,0:T(8,128)(2,1)S(1)} %get-tuple-element.144.refs_2_), channel_id=1, source_target_pairs={{0,1},{1,0},{2,3},{3,2},{4,5},{5,4},{6,7},{7,6},{8,9},{9,8},{10,11... | collective-permute-start | bytes 786440 | tf_op jit(solution)/shard_map/ppermute | solution.py:473
  46.5 10.4 %collective-permute-start.12 = (bf16[1,1024,128]{2,1,0:T(8,128)(2,1)S(1)}, bf16[1,1024,128]{2,1,0:T(8,128)(2,1)S(1)}, u32[]{:S(2)}, u32[]{:S(2)}) collective-permute-start(bf16[1,1024,128]{2,1,0:T(8,128)(2,1)S(1)} %get-tuple-element.143.refs_1_), channel_id=1, source_target_pairs={{0,1},{1,0},{2,3},{3,2},{4,5},{5,4},{6,7},{7,6},{8,9},{9,8},{10,11... | collective-permute-start | bytes 786440 | tf_op jit(solution)/shard_map/ppermute | solution.py:473
  56.3 1.5 collective-permute-start.15
  56.3 1.9 %collective-permute-start.14 = (bf16[1,1024,128]{2,1,0:T(8,128)(2,1)S(1)}, bf16[1,1024,128]{2,1,0:T(8,128)(2,1)S(1)}, u32[]{:S(2)}, u32[]{:S(2)}) collective-permute-start(bf16[1,1024,128]{2,1,0:T(8,128)(2,1)S(1)} %get-tuple-element.145.refs_3_), channel_id=1, source_target_pairs={{0,1},{1,0},{2,3},{3,2},{4,5},{5,4},{6,7},{7,6},{8,9},{9,8},{10,11... | collective-permute-start | bytes 786440 | tf_op jit(solution)/shard_map/ppermute | solution.py:473
  56.8 12.7 %collective-permute-start.10 = (bf16[176,1024]{1,0:T(8,128)(2,1)S(1)}, bf16[176,1024]{1,0:T(8,128)(2,1)S(1)}, u32[]{:S(2)}, u32[]{:S(2)}) collective-permute-start(bf16[176,1024]{1,0:T(8,128)(2,1)S(1)} %slice.12), channel_id=1, source_target_pairs={{0,32},{32,64},{64,96},{96,128},{128,160},{160,192},{192,224},{224... | collective-permute-start | bytes 1081352 | tf_op jit(solution)/shard_map/ppermute | solution.py:461
  62.5 2.0 %copy-start = (f32[1024,1024]{1,0:T(8,128)}, f32[1024,1024]{1,0:T(8,128)S(1)}, u32[]{:S(2)}) copy-start(f32[1024,1024]{1,0:T(8,128)S(1)} %product.4.later.refs_9_) | copy-start | bytes 12582916
  68.9 15.2 %collective-permute-start.17 = (bf16[1,1024,128]{2,1,0:T(8,128)(2,1)S(1)}, bf16[1,1024,128]{2,1,0:T(8,128)(2,1)S(1)}, u32[]{:S(2)}, u32[]{:S(2)}) collective-permute-start(bf16[1,1024,128]{2,1,0:T(8,128)(2,1)S(1)} %get-tuple-element.142.refs_1_), channel_id=1, source_target_pairs={{0,1},{1,0},{2,3},{3,2},{4,5},{5,4},{6,7},{7,6},{8,9},{9,8},{10,11... | collective-permute-start | bytes 786440 | tf_op jit(solution)/shard_map/ppermute | solution.py:473
  69.1 14.9 %collective-permute-start.16 = (bf16[1,1024,128]{2,1,0:T(8,128)(2,1)S(1)}, bf16[1,1024,128]{2,1,0:T(8,128)(2,1)S(1)}, u32[]{:S(2)}, u32[]{:S(2)}) collective-permute-start(bf16[1,1024,128]{2,1,0:T(8,128)(2,1)S(1)} %get-tuple-element.140.refs_0_), channel_id=1, source_target_pairs={{0,1},{1,0},{2,3},{3,2},{4,5},{5,4},{6,7},{7,6},{8,9},{9,8},{10,11... | collective-permute-start | bytes 786440 | tf_op jit(solution)/shard_map/ppermute | solution.py:473
  73.1 11.0 %collective-permute-start.18 = (bf16[1,1024,128]{2,1,0:T(8,128)(2,1)}, bf16[1,1024,128]{2,1,0:T(8,128)(2,1)S(1)}, u32[]{:S(2)}, u32[]{:S(2)}) collective-permute-start(bf16[1,1024,128]{2,1,0:T(8,128)(2,1)} %last_left.1.later.refs_2_), channel_id=1, source_target_pairs={{0,1},{1,0},{2,3},{3,2},{4,5},{5,4},{6,7},{7,6},{8,9},{9,8},{10,11... | collective-permute-start | bytes 786440 | tf_op jit(solution)/shard_map/ppermute | solution.py:473
  73.4 6.6 %collective-permute-start.19 = (bf16[80,1024]{1,0:T(8,128)(2,1)S(1)}, bf16[80,1024]{1,0:T(8,128)(2,1)S(1)}, u32[]{:S(2)}, u32[]{:S(2)}) collective-permute-start(bf16[80,1024]{1,0:T(8,128)(2,1)S(1)} %slice.13), channel_id=1, source_target_pairs={{0,224},{32,0},{64,32},{96,64},{128,96},{160,128},{192,160},{224,1... | collective-permute-start | bytes 491528 | tf_op jit(solution)/shard_map/ppermute | solution.py:465
  80.0 0.9 copy-start.2
  81.0 1.0 copy-start.5
  84.1 2.2 %copy-start.1 = (f32[1024,1024]{1,0:T(8,128)S(1)}, f32[1024,1024]{1,0:T(8,128)}, u32[]{:S(2)}) copy-start(f32[1024,1024]{1,0:T(8,128)} %copy-done) | copy-start | bytes 12582916
  86.3 0.9 copy-start.3
  91.4 63.4 %copy-start.11 = (bf16[8192,128]{1,0:T(8,128)(2,1)S(1)}, bf16[8192,128]{1,0:T(8,128)(2,1)}, u32[]{:S(2)}) copy-start(bf16[8192,128]{1,0:T(8,128)(2,1)} %x_ref.5) | copy-start | bytes 6291460
  91.4 63.4 %copy-start.12 = (bf16[128,1024]{1,0:T(8,128)(2,1)S(1)}, bf16[128,1024]{1,0:T(8,128)(2,1)}, u32[]{:S(2)}) copy-start(bf16[128,1024]{1,0:T(8,128)(2,1)} %x_ref.3) | copy-start | bytes 786436
  91.5 63.4 %copy-start.14 = (s32[2,16]{1,0:T(2,128)S(1)}, s32[2,16]{1,0:T(2,128)}, u32[]{:S(2)}) copy-start(s32[2,16]{1,0:T(2,128)} %slab_tiles.1) | copy-start | bytes 388
  91.5 63.4 %copy-start.15 = (s32[128,2]{0,1:T(2,128)S(1)}, s32[128,2]{0,1:T(2,128)}, u32[]{:S(2)}) copy-start(s32[128,2]{0,1:T(2,128)} %param.9) | copy-start | bytes 3076
  126.7 26.7 %all-to-all-start.4 = ((f32[128,1,1024]{2,1,0:T(1,128)}), f32[128,1,1024]{2,1,0:T(1,128)S(1)}, u32[]{:S(2)}, u32[]{:S(2)}) async-start(f32[128,1,1024]{2,1,0:T(1,128)} %get-tuple-element.155), calls=%async_computation.4 | async-start | bytes 1048576 | tf_op jit(solution)/shard_map/all_to_all | solution.py:482
  (2 other events, 1.5 us)

commit v2 on v0

--- a/solution.py
+++ b/solution.py
@@ -13,7 +13,7 @@
 CAP = 21
 SLAB_CAP = 19
 PARTS = 1
-ALL = ("z", "y", "xl", "xh")
+LAYER = ("z", "y", "xl")
 LOW = -2.75
 STEP = 13.8 / 65534.0
 
@@ -390,7 +390,7 @@
             s_ref[rows, cols] = s
             sums = sums + s
         sums = jnp.sum(sums, axis=0, keepdims=True)[None]
-        sum_ref[:, :, cols] = jnp.broadcast_to(sums, (128, 1, 256))
+        sum_ref[:, :, cols] = sums
         return 0
 
     lax.fori_loop(0, s_ref.shape[1] // 256, columns, 0)
@@ -402,7 +402,7 @@
         square_kernel,
         in_specs=[pl.BlockSpec(memory_space=pltpu.VMEM)],
         out_specs=[pl.BlockSpec(memory_space=pltpu.VMEM)] * 2,
-        out_shape=[jax.ShapeDtypeStruct((128, width), jnp.float32), jax.ShapeDtypeStruct((128, 1, width), jnp.float32)],
+        out_shape=[jax.ShapeDtypeStruct((128, width), jnp.float32), jax.ShapeDtypeStruct((1, 1, width), jnp.float32)],
         cost_estimate=pl.CostEstimate(flops=2**24, bytes_accessed=10 * 2**20, transcendentals=1024 * width),
         name="squares",
     )(q)
@@ -430,7 +430,8 @@
         codes = product(left, other_left, right, earlier, part, PARTS)
         parts.append(squares(lax.all_to_all(codes, ("y", "xl"), 0, 0, tiled=True)))
     sums = jnp.concatenate([b for _, b in parts], axis=2)
-    return [a for a, _ in parts], jnp.sum(lax.all_to_all(sums, ALL, 0, 0, tiled=True), axis=0)
+    sums = jnp.broadcast_to(sums + across(sums), (64, 1, 1024))
+    return [a for a, _ in parts], jnp.sum(lax.all_to_all(sums, LAYER, 0, 0, tiled=True), axis=0)
 
 
 def inflate(squared, sums):

time: 145 us -> 144 us (level)
    all_to_all x1, waiting for transfers between devices: 17.9 us -> 11.3 us  [exchange(): lax.all_to_all(sums, LAYER, 0, 0, tiled=True)]
    ppermute x4, starting transfers between devices: 6.8 us -> 1.55 us  [up(): return lax.ppermute(x, 'z', [(i, (i + 1) % NZ) for i in range(NZ)])]
    ppermute x4, starting transfers between devices: 9.7 us -> 14.1 us  [down(): return lax.ppermute(x, 'z', [(i, (i - 1) % NZ) for i in range(NZ)])]
    ppermute x1 -> x2, waiting for transfers between devices: 0.28 us -> 4.28 us  [across(): return lax.ppermute(x, 'xh', [(0, 1), (1, 0)])]
    ppermute x4, waiting for transfers between devices: 0.94 us -> 3.12 us  [down(): return lax.ppermute(x, 'z', [(i, (i - 1) % NZ) for i in range(NZ)])]
    ppermute x1 -> x2, starting transfers between devices: 1.95 us -> 3.45 us  [across(): return lax.ppermute(x, 'xh', [(0, 1), (1, 0)])]
  transfers between devices with their start and end apart: 18 -> 19, of which waited for: 8 -> 7; matrix products, arithmetic and copies ran while one was open for 1% -> 1% of each run, Pallas kernels for 22% -> 22%
where the time goes in v2:
time: 144 us
  Pallas kernels  42.4 us (29%)
  waiting for transfers between devices  33.8 us (23%)
  blocking collectives  31.3 us (22%)
  starting transfers between devices  28.2 us (20%)
  local copies, waits for them, and re-layouts  4.93 us (3%)
  other arithmetic  1.97 us (1%)
    all_to_all x1, blocking collectives, exchange(): parts.append(squares(lax.all_to_all(codes, ('y', 'xl'), 0, 0, tiled=True)))  31.3 us
    pallas_call x8, Pallas kernels, stage(): pl.pallas_call(functools.partial(stage_kernel, step), in_specs=[pl.BlockS...  20.2 us
    ppermute x4, starting transfers between devices, down(): return lax.ppermute(x, 'z', [(i, (i - 1) % NZ) for i in range(NZ)])  14.1 us
    ppermute x4, waiting for transfers between devices, up(): return lax.ppermute(x, 'z', [(i, (i + 1) % NZ) for i in range(NZ)])  13.6 us
    all_to_all x1, waiting for transfers between devices, exchange(): lax.all_to_all(sums, LAYER, 0, 0, tiled=True)  11.3 us
    pallas_call x2, Pallas kernels, product(): pl.pallas_call(functools.partial(product_kernel, counts, part, earlier is...  8.45 us
    all_to_all x1, starting transfers between devices, exchange(): lax.all_to_all(sums, LAYER, 0, 0, tiled=True)  7.8 us
    ppermute x2, waiting for transfers between devices, across(): return lax.ppermute(x, 'xh', [(0, 1), (1, 0)])  4.28 us
  transfers between devices with their start and end apart: 19, of which 7 were waited for; matrix products, arithmetic and copies ran while one was open for 1% of the time, Pallas kernels for 22%

profile of v2, /device:TPU:2, one launch (start us, length us, event | category | flops | bytes accessed | tf_op | source)
XLA Modules:
  0.0 143.5 jit_solution(17786123851935635365)
XLA Ops:
  0.0 2.4 %pack_slab.1.slab_ref = bf16[80,1024]{1,0:T(8,128)(2,1)} custom-call(s32[2,16]{1,0:T(2,128)} %slab_tiles.1, bf16[128,1024]{1,0:T(8,128)(2,1)} %x_ref.3), custom_call_target="tpu_custom_call" | custom-call | tf_op jit(solution)/shard_map/pack_slab/pallas_call | solution.py:125
  2.4 2.4 %collective-permute-start.4 = (bf16[80,1024]{1,0:T(8,128)(2,1)}, bf16[80,1024]{1,0:T(8,128)(2,1)S(1)}, u32[]{:S(2)}, u32[]{:S(2)}) collective-permute-start(bf16[80,1024]{1,0:T(8,128)(2,1)} %pack_slab.1.slab_ref), channel_id=1, source_target_pairs={{0,2},{2,0},{1,3},{3,1},{4,6},{6,4},{5,7},{7,5},{8,10},{10,8},{9,1... | collective-permute-start | bytes 491528 | tf_op jit(solution)/shard_map/ppermute | solution.py:420
  6.5 3.9 %pack_markov.1 = (bf16[256,1024]{1,0:T(8,128)(2,1)S(1)}, bf16[256,1024]{1,0:T(8,128)(2,1)S(1)}, bf16[16,128]{1,0:T(8,128)(2,1)S(1)}) custom-call(s32[128,2]{1,0:T(8,128)S(1)} %copy.16.tiles.flags_ref, s32[2,16]{1,0:T(2,128)} %slab_tiles.1, s32[128,2]{1,0:T(8,128)S(1)} %copy.16.tiles.flags_ref, bf16[8192,128]{1,0:T(8,128)(2,1)} %x_ref.5, ...), custom_call_target="tpu_custom_call" | custom-call | flops 8388608 | bytes 20971520 | tf_op jit(solution)/shard_map/pack_markov/pallas_call | solution.py:173
  10.5 1.4 collective-permute-start.5
  11.9 4.6 %collective-permute-start.7 = (bf16[256,1024]{1,0:T(8,128)(2,1)S(1)}, bf16[256,1024]{1,0:T(8,128)(2,1)S(1)}, u32[]{:S(2)}, u32[]{:S(2)}) collective-permute-start(bf16[256,1024]{1,0:T(8,128)(2,1)S(1)} %get-tuple-element.180), channel_id=1, source_target_pairs={{0,224},{32,0},{64,32},{96,64},{128,96},{160,128},{192,160},{224,1... | collective-permute-start | bytes 1572872 | tf_op jit(solution)/shard_map/ppermute | solution.py:416
  16.5 3.5 %own_rows.1.later.refs_0_ = bf16[1,1024,128]{2,1,0:T(8,128)(2,1)} custom-call(s32[128,2]{1,0:T(8,128)} %copy-done.2, bf16[16,128]{1,0:T(8,128)(2,1)} %copy-done.4, bf16[8192,128]{1,0:T(8,128)(2,1)} %x_ref.5), custom_call_target="tpu_custom_call" | custom-call | flops 1048576 | bytes 4194304 | tf_op jit(solution)/shard_map/own_rows/pallas_call | solution.py:197
  20.9 2.2 %stage.8 = (bf16[1,2,128,1024]{3,2,1,0:T(8,128)(2,1)S(1)}, bf16[16,128]{1,0:T(8,128)(2,1)S(1)}) custom-call(bf16[256,1024]{1,0:T(8,128)(2,1)S(1)} %get-tuple-element.181.ref.other_ref, bf16[256,1024]{1,0:T(8,128)(2,1)S(1)} %get-tuple-element.181.ref.other_ref, bf16[1,1024,128]{2,1,0:T(8,128)(2,1)S(1)} %copy-done), custom_call_target="tpu_custom_call" | custom-call | flops 8388608 | bytes 104857600 | tf_op jit(solution)/shard_map/stage/pallas_call | solution.py:271
  23.1 4.9 %collective-permute-done.5 = bf16[256,1024]{1,0:T(8,128)(2,1)S(1)} collective-permute-done((bf16[256,1024]{1,0:T(8,128)(2,1)S(1)}, bf16[256,1024]{1,0:T(8,128)(2,1)S(1)}, u32[]{:S(2)}, u32[]{:S(2)}) %collective-permute-start.5) | collective-permute-done | bytes 524320 | tf_op jit(solution)/shard_map/ppermute | solution.py:412
  28.1 3.2 %collective-permute-start.9 = (bf16[256,1024]{1,0:T(8,128)(2,1)S(1)}, bf16[256,1024]{1,0:T(8,128)(2,1)S(1)}, u32[]{:S(2)}, u32[]{:S(2)}) collective-permute-start(bf16[256,1024]{1,0:T(8,128)(2,1)S(1)} %get-tuple-element.186.ref.other_ref), channel_id=1, source_target_pairs={{0,224},{32,0},{64,32},{96,64},{128,96},{160,128},{192,160},{224,1... | collective-permute-start | bytes 1572872 | tf_op jit(solution)/shard_map/ppermute | solution.py:416
  31.3 2.8 %stage.9 = (bf16[1,2,128,1024]{3,2,1,0:T(8,128)(2,1)S(1)}, bf16[16,128]{1,0:T(8,128)(2,1)S(1)}, bf16[1,1024,128]{2,1,0:T(8,128)(2,1)S(1)}) custom-call(bf16[256,1024]{1,0:T(8,128)(2,1)S(1)} %get-tuple-element.187.ref.other_ref, bf16[256,1024]{1,0:T(8,128)(2,1)S(1)} %get-tuple-element.187.ref.other_ref, bf16[16,128]{1,0:T(8,128)(2,1)S(1)} %get-tuple-element.135.later), custom_call_target="tpu_custom_call" | custom-call | flops 8388608 | bytes 104857600 | tf_op jit(solution)/shard_map/stage/pallas_call | solution.py:271
  34.1 2.8 %stage.10 = (bf16[1,2,128,1024]{3,2,1,0:T(8,128)(2,1)S(1)}, bf16[16,128]{1,0:T(8,128)(2,1)S(1)}, bf16[1,1024,128]{2,1,0:T(8,128)(2,1)S(1)}) custom-call(bf16[256,1024]{1,0:T(8,128)(2,1)S(1)} %get-tuple-element.186.ref.other_ref, bf16[256,1024]{1,0:T(8,128)(2,1)S(1)} %get-tuple-element.186.ref.other_ref, bf16[16,128]{1,0:T(8,128)(2,1)S(1)} %get-tuple-element.137.later), custom_call_target="tpu_custom_call" | custom-call | flops 8388608 | bytes 104857600 | tf_op jit(solution)/shard_map/stage/pallas_call | solution.py:271
  36.9 5.3 %collective-permute-done.6 = bf16[256,1024]{1,0:T(8,128)(2,1)S(1)} collective-permute-done((bf16[256,1024]{1,0:T(8,128)(2,1)S(1)}, bf16[256,1024]{1,0:T(8,128)(2,1)S(1)}, u32[]{:S(2)}, u32[]{:S(2)}) %collective-permute-start.6) | collective-permute-done | bytes 524320 | tf_op jit(solution)/shard_map/ppermute | solution.py:412
  42.2 3.0 %collective-permute-start.10 = (bf16[256,1024]{1,0:T(8,128)(2,1)S(1)}, bf16[256,1024]{1,0:T(8,128)(2,1)S(1)}, u32[]{:S(2)}, u32[]{:S(2)}) collective-permute-start(bf16[256,1024]{1,0:T(8,128)(2,1)S(1)} %get-tuple-element.184.ref.other_ref), channel_id=1, source_target_pairs={{0,224},{32,0},{64,32},{96,64},{128,96},{160,128},{192,160},{224,1... | collective-permute-start | bytes 1572872 | tf_op jit(solution)/shard_map/ppermute | solution.py:416
  45.7 2.8 %stage.11 = (bf16[1,2,128,1024]{3,2,1,0:T(8,128)(2,1)S(1)}, bf16[16,128]{1,0:T(8,128)(2,1)S(1)}, bf16[1,1024,128]{2,1,0:T(8,128)(2,1)S(1)}) custom-call(bf16[256,1024]{1,0:T(8,128)(2,1)S(1)} %get-tuple-element.185.ref.other_ref, bf16[256,1024]{1,0:T(8,128)(2,1)S(1)} %get-tuple-element.185.ref.other_ref, bf16[16,128]{1,0:T(8,128)(2,1)S(1)} %get-tuple-element.138.later), custom_call_target="tpu_custom_call" | custom-call | flops 8388608 | bytes 104857600 | tf_op jit(solution)/shard_map/stage/pallas_call | solution.py:271
  48.5 2.8 %stage.12 = (bf16[1,2,128,1024]{3,2,1,0:T(8,128)(2,1)S(1)}, bf16[16,128]{1,0:T(8,128)(2,1)S(1)}, bf16[1,1024,128]{2,1,0:T(8,128)(2,1)S(1)}) custom-call(bf16[256,1024]{1,0:T(8,128)(2,1)S(1)} %get-tuple-element.184.ref.other_ref, bf16[256,1024]{1,0:T(8,128)(2,1)S(1)} %get-tuple-element.184.ref.other_ref, bf16[16,128]{1,0:T(8,128)(2,1)S(1)} %get-tuple-element.139.later), custom_call_target="tpu_custom_call" | custom-call | flops 8388608 | bytes 104857600 | tf_op jit(solution)/shard_map/stage/pallas_call | solution.py:271
  51.2 3.1 %collective-permute-done.10 = bf16[256,1024]{1,0:T(8,128)(2,1)S(1)} collective-permute-done((bf16[256,1024]{1,0:T(8,128)(2,1)S(1)}, bf16[256,1024]{1,0:T(8,128)(2,1)S(1)}, u32[]{:S(2)}, u32[]{:S(2)}) %collective-permute-start.10) | collective-permute-done | bytes 524320 | tf_op jit(solution)/shard_map/ppermute | solution.py:416
  54.4 3.4 %collective-permute-done.8 = bf16[256,1024]{1,0:T(8,128)(2,1)S(1)} collective-permute-done((bf16[256,1024]{1,0:T(8,128)(2,1)S(1)}, bf16[256,1024]{1,0:T(8,128)(2,1)S(1)}, u32[]{:S(2)}, u32[]{:S(2)}) %collective-permute-start.8) | collective-permute-done | bytes 524320 | tf_op jit(solution)/shard_map/ppermute | solution.py:412
  58.0 3.3 %collective-permute-start.12 = (bf16[80,1024]{1,0:T(8,128)(2,1)S(1)}, bf16[80,1024]{1,0:T(8,128)(2,1)S(1)}, u32[]{:S(2)}, u32[]{:S(2)}) collective-permute-start(bf16[80,1024]{1,0:T(8,128)(2,1)S(1)} %slice.13), channel_id=1, source_target_pairs={{0,224},{32,0},{64,32},{96,64},{128,96},{160,128},{192,160},{224,1... | collective-permute-start | bytes 491528 | tf_op jit(solution)/shard_map/ppermute | solution.py:416
  61.3 4.3 %product.4.later.refs_9_ = f32[1024,1024]{1,0:T(8,128)S(1)} custom-call(bf16[1,1024,128]{2,1,0:T(8,128)(2,1)S(1)} %copy-done.1, bf16[1,1024,128]{2,1,0:T(8,128)(2,1)S(1)} %get-tuple-element.144.refs_1_, bf16[1,1024,128]{2,1,0:T(8,128)(2,1)S(1)} %get-tuple-element.145.refs_2_, bf16[1,1024,128]{2,1,0:T(8,128)(2,1)S(1)} %get-tuple-element.146.refs_3_, ...), custom_call_target="tpu_custom_call" | custom-call | flops 2684354560 | bytes 10485760 | tf_op jit(solution)/shard_map/product/pallas_call | solution.py:360
  65.6 2.0 %stage.13 = (bf16[1,2,128,1024]{3,2,1,0:T(8,128)(2,1)S(1)}, bf16[16,128]{1,0:T(8,128)(2,1)S(1)}, bf16[1,1024,128]{2,1,0:T(8,128)(2,1)S(1)}) custom-call(bf16[256,1024]{1,0:T(8,128)(2,1)S(1)} %get-tuple-element.183.ref.other_ref, bf16[256,1024]{1,0:T(8,128)(2,1)S(1)} %get-tuple-element.183.ref.other_ref, bf16[16,128]{1,0:T(8,128)(2,1)S(1)} %get-tuple-element.140.later), custom_call_target="tpu_custom_call" | custom-call | flops 8388608 | bytes 104857600 | tf_op jit(solution)/shard_map/stage/pallas_call | solution.py:271
  67.5 2.5 %stage.14 = (bf16[1,2,128,1024]{3,2,1,0:T(8,128)(2,1)S(1)}, bf16[16,128]{1,0:T(8,128)(2,1)}, bf16[1,1024,128]{2,1,0:T(8,128)(2,1)S(1)}) custom-call(bf16[256,1024]{1,0:T(8,128)(2,1)S(1)} %get-tuple-element.182.ref.other_ref, bf16[256,1024]{1,0:T(8,128)(2,1)S(1)} %get-tuple-element.182.ref.other_ref, bf16[16,128]{1,0:T(8,128)(2,1)S(1)} %get-tuple-element.142.later), custom_call_target="tpu_custom_call" | custom-call | flops 8388608 | bytes 104857600 | tf_op jit(solution)/shard_map/stage/pallas_call | solution.py:271
  70.6 2.5 %stage.15 = (bf16[1,2,128,1024]{3,2,1,0:T(8,128)(2,1)S(1)}, bf16[16,128]{1,0:T(8,128)(2,1)}, bf16[1,1024,128]{2,1,0:T(8,128)(2,1)S(1)}) custom-call(bf16[176,1024]{1,0:T(8,128)(2,1)S(1)} %collective-permute-done.11.ref, bf16[80,1024]{1,0:T(8,128)(2,1)S(1)} %collective-permute-done.12.other_ref, f32[1024,1024]{1,0:T(8,128)S(1)} %product.4.later.refs_9_), custom_call_target="tpu_custom_call" | custom-call | flops 8388608 | bytes 104857600 | tf_op jit(solution)/shard_map/stage/pallas_call | solution.py:271
  73.3 1.4 collective-permute-done.20.refs_5_
  74.7 4.2 %product.5 = s16[8,128,1024]{2,1,0:T(8,128)(2,1)S(1)} custom-call(bf16[1,1024,128]{2,1,0:T(8,128)(2,1)S(1)} %get-tuple-element.141.refs_0_, bf16[1,1024,128]{2,1,0:T(8,128)(2,1)S(1)} %get-tuple-element.143.refs_1_, bf16[1,1024,128]{2,1,0:T(8,128)(2,1)S(1)} %get-tuple-element.153.refs_2_, bf16[1,1024,128]{2,1,0:T(8,128)(2,1)S(1)} %collective-permute-done.18.refs_3_, ...), custom_call_target="tpu_custom_call" | custom-call | flops 1610612736 | bytes 10485760 | tf_op jit(solution)/shard_map/product/pallas_call | solution.py:360
  78.9 31.3 %all_to_all.24.q_ref = s16[8,128,1024]{2,1,0:T(8,128)(2,1)} all-to-all(s16[8,128,1024]{2,1,0:T(8,128)(2,1)S(1)} %product.5), channel_id=1, replica_groups=mesh['z'=8,'y'=4,'xl'=2,'xh'=2,'core'=2] {'y','xl'}, dimensions={0} | all-to-all | bytes 4194304 | tf_op jit(solution)/shard_map/all_to_all | solution.py:431
  110.3 3.9 %squares.3 = (f32[128,1024]{1,0:T(8,128)}, f32[1,1,1024]{2,1,0:T(1,128)}) custom-call(s16[8,128,1024]{2,1,0:T(8,128)(2,1)} %all_to_all.24.q_ref), custom_call_target="tpu_custom_call" | custom-call | flops 16777216 | bytes 10485760 | tf_op jit(solution)/shard_map/squares/pallas_call | solution.py:401
  114.2 1.0 collective-permute-start.21
  115.2 4.3 %collective-permute-done.21 = f32[1,1,1024]{2,1,0:T(1,128)S(1)} collective-permute-done((f32[1,1,1024]{2,1,0:T(1,128)}, f32[1,1,1024]{2,1,0:T(1,128)S(1)}, u32[]{:S(2)}, u32[]{:S(2)}) %collective-permute-start.21) | collective-permute-done | bytes 4128 | tf_op jit(solution)/shard_map/ppermute | solution.py:420
  121.1 7.8 %all-to-all-start.4 = ((f32[64,1,1024]{2,1,0:T(1,128)}), f32[64,1,1024]{2,1,0:T(1,128)S(1)}, u32[]{:S(2)}, u32[]{:S(2)}) async-start(f32[64,1,1024]{2,1,0:T(1,128)} %broadcast_in_dim.23), calls=%async_computation.4 | async-start | bytes 524288 | tf_op jit(solution)/shard_map/all_to_all | solution.py:434
  128.9 11.3 %all-to-all-done.4 = f32[64,1,1024]{2,1,0:T(1,128)S(1)} async-done(((f32[64,1,1024]{2,1,0:T(1,128)}), f32[64,1,1024]{2,1,0:T(1,128)S(1)}, u32[]{:S(2)}, u32[]{:S(2)}) %all-to-all-start.4) | async-done | bytes 262176 | tf_op jit(solution)/shard_map/all_to_all | solution.py:434
  141.6 1.1 conditional.1
  141.6 1.1 broadcast_divide_fusion.1
  (55 shorter events, 7.3 us)
Async XLA Ops:
  2.4 8.1 %collective-permute-start.4 = (bf16[80,1024]{1,0:T(8,128)(2,1)}, bf16[80,1024]{1,0:T(8,128)(2,1)S(1)}, u32[]{:S(2)}, u32[]{:S(2)}) collective-permute-start(bf16[80,1024]{1,0:T(8,128)(2,1)} %pack_slab.1.slab_ref), channel_id=1, source_target_pairs={{0,2},{2,0},{1,3},{3,1},{4,6},{6,4},{5,7},{7,5},{8,10},{10,8},{9,1... | collective-permute-start | bytes 491528 | tf_op jit(solution)/shard_map/ppermute | solution.py:420
  5.6 0.9 copy-start.3
  6.5 10.0 %copy-start.2 = (s32[128,2]{1,0:T(8,128)}, s32[128,2]{1,0:T(8,128)S(1)}, u32[]{:S(2)}) copy-start(s32[128,2]{1,0:T(8,128)S(1)} %copy.16.tiles.flags_ref) | copy-start | bytes 3076
  10.4 1.4 %copy-start.4 = (bf16[16,128]{1,0:T(8,128)(2,1)}, bf16[16,128]{1,0:T(8,128)(2,1)S(1)}, u32[]{:S(2)}) copy-start(bf16[16,128]{1,0:T(8,128)(2,1)S(1)} %get-tuple-element.134.poison_ref) | copy-start | bytes 12292
  10.5 17.5 %collective-permute-start.5 = (bf16[256,1024]{1,0:T(8,128)(2,1)S(1)}, bf16[256,1024]{1,0:T(8,128)(2,1)S(1)}, u32[]{:S(2)}, u32[]{:S(2)}) collective-permute-start(bf16[256,1024]{1,0:T(8,128)(2,1)S(1)} %get-tuple-element.181.ref.other_ref), channel_id=1, source_target_pairs={{0,32},{32,64},{64,96},{96,128},{128,160},{160,192},{192,224},{224... | collective-permute-start | bytes 1572872 | tf_op jit(solution)/shard_map/ppermute | solution.py:412
  11.9 16.1 %collective-permute-start.7 = (bf16[256,1024]{1,0:T(8,128)(2,1)S(1)}, bf16[256,1024]{1,0:T(8,128)(2,1)S(1)}, u32[]{:S(2)}, u32[]{:S(2)}) collective-permute-start(bf16[256,1024]{1,0:T(8,128)(2,1)S(1)} %get-tuple-element.180), channel_id=1, source_target_pairs={{0,224},{32,0},{64,32},{96,64},{128,96},{160,128},{192,160},{224,1... | collective-permute-start | bytes 1572872 | tf_op jit(solution)/shard_map/ppermute | solution.py:416
  20.0 1.0 copy-start
  20.9 40.3 %copy-start.1 = (bf16[1,1024,128]{2,1,0:T(8,128)(2,1)S(1)}, bf16[1,1024,128]{2,1,0:T(8,128)(2,1)}, u32[]{:S(2)}) copy-start(bf16[1,1024,128]{2,1,0:T(8,128)(2,1)} %own_rows.1.later.refs_0_) | copy-start | bytes 786436
  28.0 14.2 %collective-permute-start.6 = (bf16[256,1024]{1,0:T(8,128)(2,1)S(1)}, bf16[256,1024]{1,0:T(8,128)(2,1)S(1)}, u32[]{:S(2)}, u32[]{:S(2)}) collective-permute-start(bf16[256,1024]{1,0:T(8,128)(2,1)S(1)} %get-tuple-element.187.ref.other_ref), channel_id=1, source_target_pairs={{0,32},{32,64},{64,96},{96,128},{128,160},{160,192},{192,224},{224... | collective-permute-start | bytes 1572872 | tf_op jit(solution)/shard_map/ppermute | solution.py:412
  28.1 14.1 %collective-permute-start.9 = (bf16[256,1024]{1,0:T(8,128)(2,1)S(1)}, bf16[256,1024]{1,0:T(8,128)(2,1)S(1)}, u32[]{:S(2)}, u32[]{:S(2)}) collective-permute-start(bf16[256,1024]{1,0:T(8,128)(2,1)S(1)} %get-tuple-element.186.ref.other_ref), channel_id=1, source_target_pairs={{0,224},{32,0},{64,32},{96,64},{128,96},{160,128},{192,160},{224,1... | collective-permute-start | bytes 1572872 | tf_op jit(solution)/shard_map/ppermute | solution.py:416
  42.2 12.2 %collective-permute-start.10 = (bf16[256,1024]{1,0:T(8,128)(2,1)S(1)}, bf16[256,1024]{1,0:T(8,128)(2,1)S(1)}, u32[]{:S(2)}, u32[]{:S(2)}) collective-permute-start(bf16[256,1024]{1,0:T(8,128)(2,1)S(1)} %get-tuple-element.184.ref.other_ref), channel_id=1, source_target_pairs={{0,224},{32,0},{64,32},{96,64},{128,96},{160,128},{192,160},{224,1... | collective-permute-start | bytes 1572872 | tf_op jit(solution)/shard_map/ppermute | solution.py:416
  45.2 12.6 %collective-permute-start.8 = (bf16[256,1024]{1,0:T(8,128)(2,1)S(1)}, bf16[256,1024]{1,0:T(8,128)(2,1)S(1)}, u32[]{:S(2)}, u32[]{:S(2)}) collective-permute-start(bf16[256,1024]{1,0:T(8,128)(2,1)S(1)} %get-tuple-element.185.ref.other_ref), channel_id=1, source_target_pairs={{0,32},{32,64},{64,96},{96,128},{128,160},{160,192},{192,224},{224... | collective-permute-start | bytes 1572872 | tf_op jit(solution)/shard_map/ppermute | solution.py:412
  45.2 12.7 %collective-permute-start.13 = (bf16[1,1024,128]{2,1,0:T(8,128)(2,1)}, bf16[1,1024,128]{2,1,0:T(8,128)(2,1)S(1)}, u32[]{:S(2)}, u32[]{:S(2)}) collective-permute-start(bf16[1,1024,128]{2,1,0:T(8,128)(2,1)} %own_rows.1.later.refs_0_), channel_id=1, source_target_pairs={{0,1},{1,0},{2,3},{3,2},{4,5},{5,4},{6,7},{7,6},{8,9},{9,8},{10,11... | collective-permute-start | bytes 786440 | tf_op jit(solution)/shard_map/ppermute | solution.py:424
  45.2 12.8 %collective-permute-start.15 = (bf16[1,1024,128]{2,1,0:T(8,128)(2,1)S(1)}, bf16[1,1024,128]{2,1,0:T(8,128)(2,1)S(1)}, u32[]{:S(2)}, u32[]{:S(2)}) collective-permute-start(bf16[1,1024,128]{2,1,0:T(8,128)(2,1)S(1)} %get-tuple-element.145.refs_2_), channel_id=1, source_target_pairs={{0,1},{1,0},{2,3},{3,2},{4,5},{5,4},{6,7},{7,6},{8,9},{9,8},{10,11... | collective-permute-start | bytes 786440 | tf_op jit(solution)/shard_map/ppermute | solution.py:424
  45.7 15.6 %collective-permute-start.14 = (bf16[1,1024,128]{2,1,0:T(8,128)(2,1)S(1)}, bf16[1,1024,128]{2,1,0:T(8,128)(2,1)S(1)}, u32[]{:S(2)}, u32[]{:S(2)}) collective-permute-start(bf16[1,1024,128]{2,1,0:T(8,128)(2,1)S(1)} %get-tuple-element.144.refs_1_), channel_id=1, source_target_pairs={{0,1},{1,0},{2,3},{3,2},{4,5},{5,4},{6,7},{7,6},{8,9},{9,8},{10,11... | collective-permute-start | bytes 786440 | tf_op jit(solution)/shard_map/ppermute | solution.py:424
  54.4 6.9 %collective-permute-start.17 = (bf16[1,1024,128]{2,1,0:T(8,128)(2,1)S(1)}, bf16[1,1024,128]{2,1,0:T(8,128)(2,1)S(1)}, u32[]{:S(2)}, u32[]{:S(2)}) collective-permute-start(bf16[1,1024,128]{2,1,0:T(8,128)(2,1)S(1)} %get-tuple-element.147.refs_4_), channel_id=1, source_target_pairs={{0,1},{1,0},{2,3},{3,2},{4,5},{5,4},{6,7},{7,6},{8,9},{9,8},{10,11... | collective-permute-start | bytes 786440 | tf_op jit(solution)/shard_map/ppermute | solution.py:424
  57.8 3.5 %collective-permute-start.16 = (bf16[1,1024,128]{2,1,0:T(8,128)(2,1)S(1)}, bf16[1,1024,128]{2,1,0:T(8,128)(2,1)S(1)}, u32[]{:S(2)}, u32[]{:S(2)}) collective-permute-start(bf16[1,1024,128]{2,1,0:T(8,128)(2,1)S(1)} %get-tuple-element.146.refs_3_), channel_id=1, source_target_pairs={{0,1},{1,0},{2,3},{3,2},{4,5},{5,4},{6,7},{7,6},{8,9},{9,8},{10,11... | collective-permute-start | bytes 786440 | tf_op jit(solution)/shard_map/ppermute | solution.py:424
  57.8 12.8 %collective-permute-start.11 = (bf16[176,1024]{1,0:T(8,128)(2,1)S(1)}, bf16[176,1024]{1,0:T(8,128)(2,1)S(1)}, u32[]{:S(2)}, u32[]{:S(2)}) collective-permute-start(bf16[176,1024]{1,0:T(8,128)(2,1)S(1)} %slice.12), channel_id=1, source_target_pairs={{0,32},{32,64},{64,96},{96,128},{128,160},{160,192},{192,224},{224... | collective-permute-start | bytes 1081352 | tf_op jit(solution)/shard_map/ppermute | solution.py:412
  58.0 12.7 %collective-permute-start.12 = (bf16[80,1024]{1,0:T(8,128)(2,1)S(1)}, bf16[80,1024]{1,0:T(8,128)(2,1)S(1)}, u32[]{:S(2)}, u32[]{:S(2)}) collective-permute-start(bf16[80,1024]{1,0:T(8,128)(2,1)S(1)} %slice.13), channel_id=1, source_target_pairs={{0,224},{32,0},{64,32},{96,64},{128,96},{160,128},{192,160},{224,1... | collective-permute-start | bytes 491528 | tf_op jit(solution)/shard_map/ppermute | solution.py:416
  70.0 3.3 %collective-permute-start.19 = (bf16[1,1024,128]{2,1,0:T(8,128)(2,1)S(1)}, bf16[1,1024,128]{2,1,0:T(8,128)(2,1)S(1)}, u32[]{:S(2)}, u32[]{:S(2)}) collective-permute-start(bf16[1,1024,128]{2,1,0:T(8,128)(2,1)S(1)} %get-tuple-element.143.refs_1_), channel_id=1, source_target_pairs={{0,1},{1,0},{2,3},{3,2},{4,5},{5,4},{6,7},{7,6},{8,9},{9,8},{10,11... | collective-permute-start | bytes 786440 | tf_op jit(solution)/shard_map/ppermute | solution.py:424
  70.1 3.2 %collective-permute-start.18 = (bf16[1,1024,128]{2,1,0:T(8,128)(2,1)S(1)}, bf16[1,1024,128]{2,1,0:T(8,128)(2,1)S(1)}, u32[]{:S(2)}, u32[]{:S(2)}) collective-permute-start(bf16[1,1024,128]{2,1,0:T(8,128)(2,1)S(1)} %get-tuple-element.141.refs_0_), channel_id=1, source_target_pairs={{0,1},{1,0},{2,3},{3,2},{4,5},{5,4},{6,7},{7,6},{8,9},{9,8},{10,11... | collective-permute-start | bytes 786440 | tf_op jit(solution)/shard_map/ppermute | solution.py:424
  73.1 1.6 %collective-permute-start.20 = (bf16[1,1024,128]{2,1,0:T(8,128)(2,1)S(1)}, bf16[1,1024,128]{2,1,0:T(8,128)(2,1)S(1)}, u32[]{:S(2)}, u32[]{:S(2)}) collective-permute-start(bf16[1,1024,128]{2,1,0:T(8,128)(2,1)S(1)} %get-tuple-element.153.refs_2_), channel_id=1, source_target_pairs={{0,1},{1,0},{2,3},{3,2},{4,5},{5,4},{6,7},{7,6},{8,9},{9,8},{10,11... | collective-permute-start | bytes 786440 | tf_op jit(solution)/shard_map/ppermute | solution.py:424
  78.9 62.7 %copy-start.5 = (bf16[8192,128]{1,0:T(8,128)(2,1)S(1)}, bf16[8192,128]{1,0:T(8,128)(2,1)}, u32[]{:S(2)}) copy-start(bf16[8192,128]{1,0:T(8,128)(2,1)} %x_ref.5) | copy-start | bytes 6291460
  78.9 62.7 %copy-start.6 = (bf16[128,1024]{1,0:T(8,128)(2,1)S(1)}, bf16[128,1024]{1,0:T(8,128)(2,1)}, u32[]{:S(2)}) copy-start(bf16[128,1024]{1,0:T(8,128)(2,1)} %x_ref.3) | copy-start | bytes 786436
  78.9 62.6 %copy-start.8 = (s32[2,16]{1,0:T(2,128)S(1)}, s32[2,16]{1,0:T(2,128)}, u32[]{:S(2)}) copy-start(s32[2,16]{1,0:T(2,128)} %slab_tiles.1) | copy-start | bytes 388
  78.9 62.6 %copy-start.9 = (s32[128,2]{0,1:T(2,128)S(1)}, s32[128,2]{0,1:T(2,128)}, u32[]{:S(2)}) copy-start(s32[128,2]{0,1:T(2,128)} %param.9) | copy-start | bytes 3076
  114.2 5.3 %collective-permute-start.21 = (f32[1,1,1024]{2,1,0:T(1,128)}, f32[1,1,1024]{2,1,0:T(1,128)S(1)}, u32[]{:S(2)}, u32[]{:S(2)}) collective-permute-start(f32[1,1,1024]{2,1,0:T(1,128)} %get-tuple-element.157), channel_id=1, source_target_pairs={{0,2},{2,0},{1,3},{3,1},{4,6},{6,4},{5,7},{7,5},{8,10},{10,8},{9,1... | collective-permute-start | bytes 12296 | tf_op jit(solution)/shard_map/ppermute | solution.py:420
  121.1 19.1 %all-to-all-start.4 = ((f32[64,1,1024]{2,1,0:T(1,128)}), f32[64,1,1024]{2,1,0:T(1,128)S(1)}, u32[]{:S(2)}, u32[]{:S(2)}) async-start(f32[64,1,1024]{2,1,0:T(1,128)} %broadcast_in_dim.23), calls=%async_computation.4 | async-start | bytes 524288 | tf_op jit(solution)/shard_map/all_to_all | solution.py:434
  142.7 0.8 copy-start.7
